TPU v7x, 32 devices: a whole 2x2x4 slice. The times are simulated.
32 devices in a mesh: box: 8 (over z, y), orb: 4 (over x, core).
Axes of the slice: x: 2, y: 2, z: 4, core: 2. Of those that a mesh axis runs over, the one named last changes fastest.
Arguments:
- orbitals: bfloat16 [16, 1000, 1536], P('box', None, 'orb'), may hold values from -0.0546875 to 0.0546875
- potential: float32 [16, 1000], P('box'), may hold values from -3 to 1
- deriv_blocks: bfloat16 [3, 10, 10], replicated, may hold values from -1 to 1
- levels: int32 [16], P('box'), may hold values from 0 to 2
- box_counts: int32 [8], P('box'), may hold values from 1 to 2, as said below
- neighbours: int32 [16, 3, 2], P('box'), may hold values from -1 to 15, as said below
Outputs:
- fock: float32 [1536, 1536], P('box', 'orb')
- correlation: float32 [1536, 1536], P('box', 'orb')
- inverse_root: float32 [1536, 1536], P('box', 'orb')
Inputs may be any that keep to these rules, and one draw needn't show every extreme that they name: Each index of box holds box_counts of live slots, which are its first slots; the counts sum to 12, and some index holds 2. `neighbours`: an entry is -1 or the global slot of a live slot, other than the slot itself, on the same index of box or on the index just before or just after it; every entry of a non-live slot is -1.
All inputs are finite; a program needn't handle non-finite values.
Results may differ from a plain program's by a relative error of at most 0.0012.
Values may be sent and summed in bfloat16 or wider, within the bound.
No kernel may reach another device: no remote copies, remote signals or barrier semaphores. Data moves between devices by JAX's collectives and lax.ppermute only.
A program may use at most 128 MiB of HBM per device.

v0:
```python
import functools

import jax
import jax.numpy as jnp
import numpy as np
from jax import lax
from jax.experimental import pallas as pl
from jax.experimental.pallas import tpu as pltpu
from jax.sharding import Mesh, PartitionSpec as P

PAIR = 2
ROWS = 16
BOX = ("lvl", "pair")
f32, bf16 = jnp.float32, jnp.bfloat16


def swap(value, axis, bit):
    count = lax.axis_size(axis)
    return lax.ppermute(value, axis, [(i, i ^ bit) for i in range(count)])


def trade(value, axis, start):
    pairs = [(i, i + 1) for i in range(start, lax.axis_size(axis) - 1, 2)]
    return lax.ppermute(value, axis, pairs + [(b, a) for a, b in pairs])


def matmul(left, right):
    return jnp.dot(left, right, preferred_element_type=f32)


def params(mebibytes):
    return pltpu.CompilerParams(vmem_limit_bytes=mebibytes * 1024 * 1024)


def pack_kernel(meta, neighbours, levels, orbitals, pot, theirs, mine):
    slots, coefficients, width = orbitals.shape
    half, fold = width // PAIR, coefficients // 2
    first = meta[0] == 0
    place = lax.broadcasted_iota(jnp.int32, (8, width), 1)
    for slot in range(slots):
        keep = slot < meta[1]
        for part in range(2):
            here = orbitals[slot, part * fold : (part + 1) * fold, :]
            here = jnp.where(keep, here, jnp.zeros_like(here))
            low, high = here[:, :half], here[:, half:]
            lanes = slice(part * half, (part + 1) * half)
            theirs[slot, :fold, lanes] = jnp.where(first, high, low)
            mine[slot, :fold, lanes] = jnp.where(first, low, high)
        own_id = meta[2] + slot
        facts = jnp.where(place == 6, levels[slot], jnp.where(place == 7, jnp.where(keep, 1, 0), 0))
        for c in range(6):
            target = neighbours[slot, c // 2, c % 2]
            facts = jnp.where(place == c, jnp.where(target >= 0, target - own_id, 16 * slots), facts)
        facts = facts.astype(f32).astype(bf16)
        for packed in (theirs, mine):
            packed[slot, fold : fold + 1, :] = facts[:1]
        row = fold + 1
        for start in range(0, pot.shape[1], width):
            stop = min(start + width, pot.shape[1])
            exact = pot[slot : slot + 1, start:stop]
            for _ in range(3):
                part = exact.astype(bf16)
                exact = exact - part.astype(f32)
                for packed in (theirs, mine):
                    packed[slot, row : row + 1, : stop - start] = part
                    if stop - start < width:
                        packed[slot, row : row + 1, stop - start :] = jnp.zeros((1, width - stop + start), bf16)
                row += 1
        for packed in (theirs, mine):
            packed[slot, row:, :] = jnp.zeros((packed.shape[1] - row, width), bf16)


def pack(meta, neighbours, levels, orbitals, pot):
    slots, coefficients, width = orbitals.shape
    fold = coefficients // 2
    padded = -(-(fold + 1 + 3 * -(-coefficients // width)) // ROWS) * ROWS
    vmem, smem = pl.BlockSpec(memory_space=pltpu.VMEM), pl.BlockSpec(memory_space=pltpu.SMEM)
    return pl.pallas_call(
        pack_kernel,
        out_shape=[jax.ShapeDtypeStruct((slots, padded, width), bf16)] * 2,
        in_specs=[smem, smem, smem, vmem, vmem],
        out_specs=[vmem, vmem],
        compiler_params=params(24),
        name="pack",
    )(meta, neighbours, levels, orbitals, pot)


def unfold_kernel(fold, meta, beside_in, rest_in, whole, top, beside, rest, sems):
    copies = [
        pltpu.make_async_copy(source, target, sems.at[i])
        for i, (source, target) in enumerate(((beside_in, beside), (rest_in, rest)))
    ]
    for copy in copies:
        copy.start()
    slots, _, width = beside.shape
    half = width // PAIR
    first = meta[0] == 0
    for copy in copies:
        copy.wait()
    for slot in range(slots):
        for part in range(2):
            lanes = slice(part * half, (part + 1) * half)
            near, far = beside[slot, :fold, lanes], rest[slot, :fold, lanes]
            start = (2 * slot + part) * fold
            here = jnp.concatenate([jnp.where(first, near, far), jnp.where(first, far, near)], axis=1)
            whole[start : start + fold, :] = here
    top[...] = whole[: top.shape[0], :]


def unfold(meta, beside, rest, fold, cut):
    slots, _, width = beside.shape
    vmem = pl.BlockSpec(memory_space=pltpu.VMEM)
    return pl.pallas_call(
        functools.partial(unfold_kernel, fold),
        out_shape=[
            jax.ShapeDtypeStruct((2 * slots * fold, width), bf16),
            jax.ShapeDtypeStruct((cut, width), bf16),
        ],
        in_specs=[pl.BlockSpec(memory_space=pltpu.SMEM)] + [pl.BlockSpec(memory_space=pltpu.HBM)] * 2,
        out_specs=[vmem, vmem],
        scratch_shapes=[
            pltpu.VMEM(beside.shape, bf16),
            pltpu.VMEM(beside.shape, bf16),
            pltpu.SemaphoreType.DMA((2,)),
        ],
        compiler_params=params(24),
        name="unfold",
    )(meta, beside, rest)


def load_left(lefts, held, sems):
    copies = []
    for q, pieces in enumerate(lefts):
        row = 0
        for piece in pieces:
            rows, width = piece.shape
            here = held.at[row : row + rows, q * width : (q + 1) * width]
            copies.append(pltpu.make_async_copy(piece, here, sems.at[len(copies)]))
            row += rows
    for copy in copies:
        copy.start()
    return copies


def grouped(refs, counts):
    refs = list(refs)
    return [[refs.pop(0) for _ in range(count)] for count in counts]


def correlation_kernel(share, counts, meta, *refs):
    refs, (out, held, turned, sems) = refs[:-4], refs[-4:]
    groups, half, width = out.shape
    lefts, before = grouped(refs, counts), refs[sum(counts) :]
    copies = load_left(lefts, held, sems)
    first = meta[0] == 0
    for copy in copies[: counts[0]]:
        copy.wait()
    own = held[:, :width]
    own = jnp.where(first, own[:, :half], own[:, half:]).T
    live = lax.broadcasted_iota(jnp.int32, own.shape, 1) < meta[1 if before else 2]
    turned[...] = jnp.where(live, own, jnp.zeros_like(own))
    for base in range(0, groups, 2):
        for copy in copies[max(sum(counts[:base]), counts[0]) : sum(counts[: base + 2])]:
            copy.wait()
        wide = matmul(turned[...], held[:, base * width : (base + 2) * width])
        for q in (base, base + 1):
            total = wide[:, (q - base) * width : (q - base + 1) * width]
            if before:
                total = total + before[0][q]
                if q == 0:
                    rows = lax.broadcasted_iota(jnp.int32, (half, width), 0) + jnp.where(first, 0, half)
                    columns = lax.broadcasted_iota(jnp.int32, (half, width), 1)
                    total = total - jnp.where(rows == columns, share, 0.0)
            out[q] = total.astype(out.dtype)


def box_correlation(share, meta, lefts, before, half):
    depth, width = sum(piece.shape[0] for piece in lefts[0]), lefts[0][0].shape[1]
    counts = [len(pieces) for pieces in lefts]
    vmem = pl.BlockSpec(memory_space=pltpu.VMEM)
    extra = [] if before is None else [before]
    return pl.pallas_call(
        functools.partial(correlation_kernel, share, counts),
        out_shape=jax.ShapeDtypeStruct((len(lefts), half, width), f32 if before is None else bf16),
        in_specs=[pl.BlockSpec(memory_space=pltpu.SMEM)]
        + [pl.BlockSpec(memory_space=pl.ANY)] * sum(counts)
        + [vmem] * len(extra),
        out_specs=vmem,
        scratch_shapes=[
            pltpu.VMEM((depth, len(lefts) * width), bf16),
            pltpu.VMEM((half, depth), bf16),
            pltpu.SemaphoreType.DMA((sum(counts),)),
        ],
        compiler_params=params(32),
        cost_estimate=pl.CostEstimate(
            flops=2 * len(lefts) * depth * width * half, bytes_accessed=2 * len(lefts) * depth * width, transcendentals=0
        ),
        name="correlation",
    )(meta, *[piece for pieces in lefts for piece in pieces], *extra)


def fock_kernel(side, counts, right, *refs):
    outs, (held, raw, turned, sems, last_sem) = refs[sum(counts) : -5], refs[-5:]
    lefts = grouped(refs, counts)
    before, apart, outs = (None, None, outs) if len(outs) == 1 else (outs[0], outs[1], outs[2:])
    out = outs[0]
    last = pltpu.make_async_copy(right.at[side], raw, last_sem)
    last.start()
    copies = load_left(lefts, held, sems)
    half, width = out.shape[-2] // (3 if before is None else 1), out.shape[-1]
    last.wait()
    turned[...] = raw[...].T
    for base in range(0, len(lefts), 2):
        for copy in copies[sum(counts[:base]) : sum(counts[: base + 2])]:
            copy.wait()
        wide = matmul(turned[...], held[:, base * width : (base + 2) * width])
        for q in (base, base + 1):
            total = wide[:, (q - base) * width : (q - base + 1) * width]
            if before is None:
                out[q] = total
                continue
            total = total + before[q]
            main = total[:half] + total[half : 2 * half]
            top = main.astype(bf16)
            parts = (top, (main - top.astype(f32)).astype(bf16), total[2 * half :].astype(bf16))

            def store(target):
                for i in range(3):
                    target[i] = parts[i]

            for distance, target in enumerate(outs):
                pl.when(q ^ apart[0] == distance)(functools.partial(store, target))


def box_fock(side, lefts, right, before, apart):
    depth, width = sum(piece.shape[0] for piece in lefts[0]), lefts[0][0].shape[1]
    counts = [len(pieces) for pieces in lefts]
    tall = right.shape[-1]
    anywhere, vmem = pl.BlockSpec(memory_space=pl.ANY), pl.BlockSpec(memory_space=pltpu.VMEM)
    extra = [] if before is None else [before, apart]
    out = jax.ShapeDtypeStruct((len(lefts), tall, width), f32)
    if before is not None:
        out = [jax.ShapeDtypeStruct((3, tall // 3, width), bf16)] * len(lefts)
    return pl.pallas_call(
        functools.partial(fock_kernel, side, counts),
        out_shape=out,
        in_specs=[anywhere] * (sum(counts) + 1) + [vmem, pl.BlockSpec(memory_space=pltpu.SMEM)][: len(extra)],
        out_specs=vmem if before is None else [vmem] * len(lefts),
        scratch_shapes=[
            pltpu.VMEM((depth, len(lefts) * width), bf16),
            pltpu.VMEM(right.shape[1:], bf16),
            pltpu.VMEM((tall, depth), bf16),
            pltpu.SemaphoreType.DMA((sum(counts),)),
            pltpu.SemaphoreType.DMA(()),
        ],
        compiler_params=params(40),
        cost_estimate=pl.CostEstimate(
            flops=2 * len(lefts) * depth * width * tall, bytes_accessed=2 * len(lefts) * depth * width, transcendentals=0
        ),
        name="fock",
    )(right, *[piece for pieces in lefts for piece in pieces], *extra)


def root_kernel(levels, meta, *refs):
    pieces, (offset, root, whole, rows_f, cols_b, sems) = refs[:-6], refs[-6:]
    level, pair, orb = meta[0], meta[1], meta[2]
    coarse, width = offset.shape
    side = whole.shape[0]
    groups = side // width
    copies = []
    for piece, (z, y, q) in zip(pieces, piece_places(levels)):
        for i in range(len(z)):
            start = ((orb ^ q) * PAIR + (pair ^ y)) * coarse
            rows = pl.ds(pl.multiple_of(start, coarse), coarse)
            lanes = pl.ds(pl.multiple_of((level ^ z[i]) * width, width), width)
            copies.append(
                pltpu.make_async_copy(
                    piece.at[i * coarse : (i + 1) * coarse], whole.at[rows, lanes], sems.at[len(copies)]
                )
            )
    for copy in copies:
        copy.start()
    for copy in copies:
        copy.wait()
    row0 = pl.multiple_of((level * PAIR + pair) * coarse, coarse)
    own_lanes = pl.ds(pl.multiple_of(orb * width, width), width)
    rows = whole[pl.ds(row0, coarse), :]

    for j in range(groups):
        lanes = slice(j * width, (j + 1) * width)
        rows_f[:, lanes] = matmul(rows, whole[:, lanes])
    columns = whole[:, own_lanes]
    for i in range(groups):
        here = slice(i * width, (i + 1) * width)
        square = matmul(whole[here, :], columns)
        cols_b[here, :] = (0.25 * (whole[here, own_lanes].astype(f32) - square)).astype(bf16)
    left = (rows.astype(f32) - 0.25 * rows_f[...]).astype(bf16)
    value = matmul(left, cols_b[...]) + 0.125 * rows_f[:, own_lanes] - 0.5 * offset[...]
    row_ids = lax.broadcasted_iota(jnp.int32, value.shape, 0) + row0
    col_ids = lax.broadcasted_iota(jnp.int32, value.shape, 1) + orb * width
    root[...] = value + jnp.where(row_ids == col_ids, 1.0, 0.0)


def piece_places(levels):
    places = []
    for core in (0, 1):
        for half in range(2):
            z = [half * levels // 2 + i for i in range(levels // 2)]
            for second in (0, 1):
                for inner in (0, 1):
                    y, far = (second, inner) if half else (inner, second)
                    places.append((z, y, 2 * far + core))
    return places


def root_of(meta, pieces, offset, side, levels):
    coarse, width = offset.shape
    vmem, anywhere = pl.BlockSpec(memory_space=pltpu.VMEM), pl.BlockSpec(memory_space=pl.ANY)
    return pl.pallas_call(
        functools.partial(root_kernel, levels),
        out_shape=jax.ShapeDtypeStruct(offset.shape, f32),
        in_specs=[pl.BlockSpec(memory_space=pltpu.SMEM)] + [anywhere] * len(pieces) + [vmem],
        out_specs=vmem,
        scratch_shapes=[
            pltpu.VMEM((side, side), bf16),
            pltpu.VMEM((coarse, side), f32),
            pltpu.VMEM((side, width), bf16),
            pltpu.SemaphoreType.DMA((side // coarse * (side // width),)),
        ],
        compiler_params=params(40),
        cost_estimate=pl.CostEstimate(flops=16 * side * side * width, bytes_accessed=4 * side * side, transcendentals=0),
        name="root",
    )(meta, *pieces, offset)


def fill_tables(slots, levels, place_meta, facts, table, scale):
    level, pair = place_meta[0], place_meta[1]
    even = lax.rem(level, 2) == 0
    none = 6 * slots

    def place(slot_id):
        box = lax.div(slot_id, slots)
        apart = lax.div(box, PAIR) - level
        base = jnp.where(apart == 0, 0, jnp.where((apart < 0) == even, 4, 2))
        return (base + jnp.where(lax.rem(box, PAIR) != pair, 1, 0)) * slots + lax.rem(slot_id, slots)

    for index in range(4 * slots):
        group, r = divmod(index, slots)

        def fact(c):
            if group < 2:
                return facts[group, r, c]
            swap_id = jnp.where(even, 1, 0) if group == 2 else jnp.where(even, 0, 1)
            near_pair = 1 if group == 2 else 0
            return facts[2 + swap_id + jnp.where(pair == near_pair, 0, 2), r, c]

        box = (
            level * PAIR + pair,
            level * PAIR + 1 - pair,
            jnp.maximum(level * PAIR - 1, 0),
            jnp.minimum((level + 1) * PAIR, levels * PAIR - 1),
        )[group]
        there = (True, True, level > 0, level < levels - 1)[group]
        own_id = box * slots + r
        own_place = place(own_id)
        table[index, 0] = jnp.where((fact(7) > 0) & there, own_place, -1)
        for a in range(3):
            for k in (0, 2):
                distance = fact(2 * a + k // 2)
                target = place(jnp.maximum(own_id + distance, 0))
                target = jnp.where(distance < 16 * slots, target, none)
                table[index, 1 + 3 * a + k] = jnp.clip(target, 0, none)
            table[index, 2 + 3 * a] = own_place
        level_of = fact(6)
        scale[index] = jnp.where(level_of == 0, 0.5, jnp.where(level_of == 1, 1.0, 2.0))


def kinetic_kernel(edge, slots, levels, place_meta, facts, *refs):
    parts, refs = refs[:6], refs[6:]
    (fwd_in, fwd_out, back_in, back_mid, back_out), out, refs = refs[:5], refs[5], refs[6:]
    raw, x, outer, inner, total, total_fix, lines, columns, table, scale, sems = refs
    square = edge * edge
    own = PAIR * slots
    padded, width = x.shape[2:]
    copies = [pltpu.make_async_copy(part, raw.at[place], sems.at[place]) for place, part in enumerate(parts)]
    for copy in copies:
        copy.start()
    tail = padded - ROWS
    x[:, :, tail:, :] = jnp.zeros((x.shape[0], edge, ROWS, width), bf16)
    x[6 * slots] = jnp.zeros((edge, padded, width), bf16)
    total[...] = jnp.zeros_like(total)
    total_fix[...] = jnp.zeros_like(total_fix)
    fill_tables(slots, levels, place_meta, facts, table, scale)
    lines[...] = jnp.zeros_like(lines)
    for copy in copies:
        copy.wait()
    lanes = raw.shape[3]
    for t in range(own):
        for start in range(0, lines.shape[1], lanes):
            row = edge * square // 2 + 1 + 3 * (start // lanes)
            high, middle, low = (
                raw[t // slots, t % slots, row + i : row + i + 1, :].astype(f32) for i in range(3)
            )
            lines[t : t + 1, start : start + lanes] = (high + middle) + low
    columns[...] = lines[...].T

    def lay_out(place, carry):
        for slot in range(slots):
            for i in range(edge):
                part, row = i // (edge // 2), i % (edge // 2) * square
                x[place * slots + slot, i, :square, :] = raw[
                    place, slot, row : row + square, part * width : (part + 1) * width
                ]
        return carry

    lax.fori_loop(0, len(parts), lay_out, 0)
    chunks = -(-square // ROWS)

    def per_slot(s, carry):
        @pl.when(table[s, 0] >= 0)
        def _():
            both_scales = 0.5 * scale[s] * scale[s]
            sums = (total, total_fix)

            def split(exact):
                exact = both_scales * exact
                value = exact.astype(bf16)
                return value, (value.astype(f32) - exact).astype(bf16)

            sources = [[table[s, 1 + 3 * a + k] for k in range(3)] for a in range(3)]
            here = sources[0][1]

            def forward(a):
                if a == 0:
                    for i in range(chunks):
                        rows = slice(i * ROWS, (i + 1) * ROWS)
                        block = [x[t, :, rows, :].reshape(edge * ROWS, width) for t in sources[0]]
                        fields = split(matmul(fwd_out[...], jnp.concatenate(block, axis=0)))
                        for field in range(2):
                            outer[field, :, rows, :] = fields[field].reshape(edge, ROWS, width)
                else:
                    for i in range(edge):
                        block = jnp.concatenate([x[t, i] for t in sources[a]], axis=0)
                        fields = split(matmul(fwd_in[a - 1], block))
                        for field in range(2):
                            inner[field, i, (a - 1) * padded : a * padded, :] = fields[field]

            def back_outer(k, target):
                for i in range(chunks):
                    rows = slice(i * ROWS, (i + 1) * ROWS)
                    for field in range(2):
                        term = matmul(back_out[k], outer[field, :, rows, :].reshape(edge * ROWS, width))
                        sums[field][target, :, rows, :] += term.reshape(edge, ROWS, width)

            @pl.when(here < own)
            def _():
                for a in range(3):
                    forward(a)
                back_outer(1, here)
                for i in range(edge):
                    for field in range(2):
                        sums[field][here, i] += matmul(back_mid[...], inner[field, i])

            for a in range(3):
                pl.when((here >= own) & ((sources[a][0] < own) | (sources[a][2] < own)))(functools.partial(forward, a))

            for k in (0, 2):
                for a in range(3):
                    target = sources[a][k]

                    @pl.when(target < own)
                    def _():
                        if a == 0:
                            back_outer(k, target)
                        else:
                            for i in range(edge):
                                for field in range(2):
                                    here = inner[field, i, (a - 1) * padded : a * padded, :]
                                    sums[field][target, i] += matmul(back_in[a - 1, k], here)

        return carry

    lax.fori_loop(0, table.shape[0], per_slot, 0)

    for t in range(own):
        for i in range(edge):
            rows = slice(i * square, (i + 1) * square)
            weighted = (columns[rows, t : t + 1] * x[t, i, :square, :].astype(f32)).astype(bf16)
            whole = total[t, i, :square, :] + weighted.astype(f32)
            top = whole.astype(bf16)
            low = (whole - top.astype(f32)).astype(bf16)
            fix = total_fix[t, i, :square, :].astype(bf16)
            out[t, rows, :] = jnp.concatenate([top, low, fix], axis=1)


def matrices_kernel(stacked, blocks, *refs):
    spots, outs = refs[:9], refs[9:]
    fwd_in, fwd_out, back_in, back_mid, back_out = outs
    for mode in range(3):
        spot, spread, same = spots[3 * mode : 3 * mode + 3]
        wide = matmul(matmul(spot[...], stacked[...]).astype(bf16), spread[...])
        wide = (wide * jnp.concatenate([same[...]] * 3, axis=1)).astype(bf16)
        if mode == 2:
            fwd_out[...] = wide
        else:
            fwd_in[mode] = wide
        for k in range(3):
            turned = lax.dot_general(spot[...], blocks[k], (((1,), (1,)), ((), ())), preferred_element_type=f32)
            turned = lax.dot_general(
                turned.astype(bf16), spot[...], (((1,), (1,)), ((), ())), preferred_element_type=f32
            )
            turned = (turned * same[...]).astype(bf16)
            if mode == 2:
                back_out[k] = turned
            else:
                back_in[mode, k] = turned
    back_mid[...] = jnp.concatenate([back_in[0, 1], back_in[1, 1]], axis=1)


def block_matrices(deriv_blocks):
    edge = deriv_blocks.shape[1]
    square = edge * edge
    padded = -(-square // ROWS) * ROWS
    tall = edge * ROWS
    ids = np.arange(padded)
    slow = ((ids[:, None] // edge) == np.arange(edge)).astype(np.float32)
    fast = (((ids[:, None] % edge) == np.arange(edge)) & (ids[:, None] < square)).astype(np.float32)
    ids = np.arange(tall)
    outer = ((ids[:, None] // ROWS) == np.arange(edge)).astype(np.float32)
    within = ((ids[:, None] % ROWS) == np.arange(ROWS)).astype(np.float32)
    stacked = jnp.moveaxis(deriv_blocks, 0, 1).reshape(edge, 3 * edge)
    constants = []
    for spot, mask in ((slow, fast), (fast, slow), (outer, within)):
        spread = np.kron(np.eye(3, dtype=np.float32), spot.T)
        constants += [jnp.asarray(spot, bf16), jnp.asarray(spread, bf16), jnp.asarray(mask @ mask.T, f32)]
    vmem = pl.BlockSpec(memory_space=pltpu.VMEM)
    shapes = [(2, padded, 3 * padded), (tall, 3 * tall), (2, 3, padded, padded), (padded, 2 * padded), (3, tall, tall)]
    return pl.pallas_call(
        matrices_kernel,
        out_shape=[jax.ShapeDtypeStruct(shape, bf16) for shape in shapes],
        in_specs=[vmem] * 11,
        out_specs=[vmem] * 5,
        compiler_params=params(24),
        name="matrices",
    )(stacked, deriv_blocks, *constants)


def kinetic(parts, place_meta, facts, matrices, edge, coefficients, levels):
    slots, folded, lanes = parts[0].shape
    width = lanes // 2
    padded = matrices[0].shape[1]
    own = PAIR * slots
    vmem = pl.BlockSpec(memory_space=pltpu.VMEM)
    smem = pl.BlockSpec(memory_space=pltpu.SMEM)
    anywhere = pl.BlockSpec(memory_space=pl.ANY)
    return pl.pallas_call(
        functools.partial(kinetic_kernel, edge, slots, levels),
        out_shape=jax.ShapeDtypeStruct((own, coefficients, 3 * width), bf16),
        in_specs=[smem] * 2 + [anywhere] * 6 + [vmem] * 5,
        out_specs=vmem,
        scratch_shapes=[
            pltpu.VMEM((6, slots, folded, lanes), bf16),
            pltpu.VMEM((6 * slots + 1, edge, padded, width), bf16),
            pltpu.VMEM((2, edge, padded, width), bf16),
            pltpu.VMEM((2, edge, 2 * padded, width), bf16),
            pltpu.VMEM((own, edge, padded, width), f32),
            pltpu.VMEM((own, edge, padded, width), f32),
            pltpu.VMEM((own + -own % 8, coefficients + -coefficients % lanes), f32),
            pltpu.VMEM((coefficients + -coefficients % lanes, own + -own % 8), f32),
            pltpu.SMEM((4 * slots, 10), jnp.int32),
            pltpu.SMEM((4 * slots,), f32),
            pltpu.SemaphoreType.DMA((6,)),
        ],
        compiler_params=params(48),
        cost_estimate=pl.CostEstimate(flops=2 * 10**10, bytes_accessed=40 * 10**6, transcendentals=0),
        name="kinetic",
    )(place_meta, facts, *parts, *matrices)


def offset_sum_kernel(meta, *refs):
    blocks, (small, kept, sent) = refs[:-3], refs[-3:]
    total = blocks[0][...].astype(f32)
    for block in blocks[1:]:
        total = total + block[...].astype(f32)
    small[...] = total.astype(bf16)
    half = kept.shape[0]
    first = meta[0] == 0
    low, high = total[:, :half].T, total[:, half:].T
    kept[...] = jnp.where(first, low, high)
    sent[...] = jnp.where(first, high, low)


def fock_sum_kernel(meta, *refs):
    blocks, (share, kept, sent) = refs[:-3], refs[-3:]
    sums = [sum((block[part].astype(f32) for block in blocks[1:]), blocks[0][part].astype(f32)) for part in range(3)]
    main = sums[0] + sums[1]
    share[...] = sums[2].astype(bf16)
    half = kept.shape[0]
    first = meta[0] == 0
    low, high = main[:, :half].T, main[:, half:].T
    kept[...] = jnp.where(first, low, high)
    sent[...] = jnp.where(first, high, low)


def level_sum(kernel, meta, blocks):
    tall, width = blocks[0].shape[-2:]
    vmem = pl.BlockSpec(memory_space=pltpu.VMEM)
    turned = jax.ShapeDtypeStruct((width // PAIR, tall), f32)
    return pl.pallas_call(
        kernel,
        out_shape=[jax.ShapeDtypeStruct((tall, width), bf16), turned, turned],
        in_specs=[pl.BlockSpec(memory_space=pltpu.SMEM)] + [vmem] * len(blocks),
        out_specs=[vmem] * 3,
        compiler_params=params(24),
        name="level_sum",
    )(meta, *blocks)


def body(orbitals, potential, deriv_blocks, levels, box_counts, neighbours):
    slots, coefficients, own_width = orbitals.shape
    edge = deriv_blocks.shape[1]
    level, pair, orb = lax.axis_index("lvl"), lax.axis_index("pair"), lax.axis_index("orb")
    level_count, orb_count = lax.axis_size("lvl"), lax.axis_size("orb")
    half, fold = own_width // PAIR, coefficients // 2
    all_width = own_width * orb_count
    box_rows = all_width // (level_count * PAIR)
    first = pair == 0
    groups = range(orb_count)
    square_grid = level_count == orb_count == 4 and box_rows == half
    row0, col0 = (level * PAIR + pair) * box_rows, orb * own_width

    own_base = (level * PAIR + pair) * slots
    pack_meta = jnp.stack([pair, box_counts[0], own_base]).astype(jnp.int32)
    theirs, mine = pack(pack_meta, neighbours, levels, orbitals, potential)
    active = orbitals

    far = {q: swap(active, "orb", q) for q in groups if q and q % 2 == 0}
    beside = swap(theirs, "pair", 1)
    first_mine, second_mine = trade(mine, "lvl", 0), trade(mine, "lvl", 1)
    later_mine, beside = lax.optimization_barrier((mine, beside))
    beside_rest = swap(later_mine, "pair", 1)
    first_beside, second_beside = trade(beside, "lvl", 0), trade(beside, "lvl", 1)

    matrices = block_matrices(deriv_blocks)

    def facts_of(parts):
        return jnp.stack([part[:, fold, :8] for part in parts]).astype(f32).astype(jnp.int32)

    early_facts = facts_of([mine, beside, first_mine, second_mine])
    flat = lambda block: block.reshape(-1, block.shape[-1])
    cut = -(-slots * coefficients // (2 * ROWS)) * ROWS
    beside_all, beside_top = unfold(pack_meta, beside, beside_rest, fold, cut)

    parts = [mine, beside, first_mine, first_beside, second_mine, second_beside]
    far, active, parts, beside_all, beside_top, matrices, early_facts = lax.optimization_barrier(
        (far, active, parts, beside_all, beside_top, matrices, early_facts)
    )
    facts = jnp.concatenate([early_facts, facts_of([parts[3], parts[5]])])
    cross = {q: [swap(beside_top, "orb", q), swap(flat(far[q])[cut:], "pair", 1)] for q in far}
    left_own = {0: active, 1: swap(active, "orb", 1), **far}
    left_beside = {0: [beside_all], 1: [swap(beside_all, "orb", 1)]}
    for q in far:
        left_own[q + 1] = swap(far[q], "orb", 1)

    def natural(blocks):
        return jnp.concatenate([lax.dynamic_index_in_dim(blocks, orb ^ j, keepdims=False) for j in groups], axis=1)

    def along_levels(blocks):
        mine_block = lambda target: lax.dynamic_index_in_dim(blocks, orb ^ target, keepdims=False)
        steps = range(1, level_count)
        return [mine_block(level)] + [swap(mine_block(level ^ step), "lvl", step) for step in steps]

    def both_halves(kept, got):
        return jnp.concatenate([jnp.where(first, kept, got), jnp.where(first, got, kept)], axis=1)

    def own_block(strip):
        strip = lax.all_gather(lax.psum(strip, "lvl"), ("orb", "pair"), axis=0, tiled=True)
        strip = lax.dynamic_slice_in_dim(strip, row0, box_rows, axis=0)
        return lax.dynamic_slice_in_dim(strip, col0, own_width, axis=1)

    live_rows = box_counts[0] * coefficients
    meta = jnp.stack([pair, slots * coefficients, live_rows]).astype(jnp.int32)

    place_meta = jnp.stack([level, pair]).astype(jnp.int32)
    right = kinetic(parts, place_meta, facts, matrices, edge, coefficients, level_count)

    cross, right, meta = lax.optimization_barrier((cross, right, meta))
    lefts_own = [[flat(left_own[q])] for q in groups]
    lefts_beside = dict(left_beside)
    for q in far:
        lefts_beside[q] = list(cross[q])
        lefts_beside[q + 1] = [swap(piece, "orb", 1) for piece in cross[q]]
    lefts_beside = [lefts_beside[q] for q in groups]

    share = 1.0 / level_count
    blocks = box_correlation(share, meta, lefts_own, None, half)
    blocks = box_correlation(share, meta, lefts_beside, blocks, half)
    right = right.reshape(2, slots * coefficients, 3 * half)
    fock_part = box_fock(0, lefts_own, right, None, None)
    if square_grid:
        sent = along_levels(blocks)
        sent, fock_part = lax.optimization_barrier((sent, fock_part))
        small, kept, other = level_sum(offset_sum_kernel, meta, sent)
        offset = both_halves(kept, swap(other, "pair", 1))
    else:
        offset = own_block(natural(blocks).astype(f32))
    row_ids = row0 + jnp.arange(box_rows, dtype=jnp.int32)
    col_ids = col0 + jnp.arange(own_width, dtype=jnp.int32)
    correlation = offset + (row_ids[:, None] == col_ids[None, :]).astype(f32)
    apart = (orb ^ level if square_grid else 0 * orb).reshape(1).astype(jnp.int32)
    fock_blocks = box_fock(1, lefts_beside, right, fock_part, apart)
    if square_grid:
        pieces = [small] + [swap(small, "lvl", z) for z in range(1, level_count)]
        pieces, fock_blocks, offset = lax.optimization_barrier((pieces, fock_blocks, offset))
        join = functools.partial(jnp.concatenate, axis=0)
        top, low = join(pieces[: level_count // 2]), join(pieces[level_count // 2 :])
        sent = [fock_blocks[0]] + [swap(fock_blocks[step], "lvl", step) for step in range(1, level_count)]
        got = [swap(top, "pair", 1), swap(low, "orb", 2)]
        tops, lows = [top, got[0]], [low, got[1]]
        far_tops, far_lows = [swap(piece, "orb", 2) for piece in tops], [swap(piece, "pair", 1) for piece in lows]
        far_tops[1], far_lows[1], sent = lax.optimization_barrier((far_tops[1], far_lows[1], sent))
        pieces = tops + far_tops + lows + far_lows
        pieces += [swap(piece, "orb", 1) for piece in pieces]
        root_meta = jnp.stack([level, pair, orb]).astype(jnp.int32)
        inverse_root = root_of(root_meta, pieces, offset, all_width, level_count)
        share, kept, other = level_sum(fock_sum_kernel, meta, sent)
        to = [
            ((z * PAIR + y) * orb_count + o, (o * PAIR + y) * orb_count + z)
            for z in range(level_count)
            for y in range(PAIR)
            for o in groups
        ]
        got = swap(other, "pair", 1), lax.ppermute(share, BOX + ("orb",), to)
        inverse_root, got = lax.optimization_barrier((inverse_root, got))
        fock = both_halves(kept, got[0]) + got[1].astype(f32)
    else:
        fock_blocks = jnp.stack(fock_blocks)
        main = natural(fock_blocks[:, 0]).astype(f32) + natural(fock_blocks[:, 1]).astype(f32)
        main = lax.all_gather(lax.psum(main, "lvl"), "pair", axis=0, tiled=True)
        fock = lax.dynamic_slice_in_dim(main, row0, box_rows, axis=1).T + own_block(natural(fock_blocks[:, 2]).astype(f32))
        gathered = lax.all_gather(offset.astype(bf16), "orb", axis=1, tiled=True)
        whole = lax.all_gather(gathered, BOX, axis=0, tiled=True)
        rows_of = lax.dynamic_slice_in_dim(whole, row0, box_rows, axis=0)
        cols_of = lax.dynamic_slice_in_dim(whole, col0, own_width, axis=1)
        row_square, col_square = matmul(rows_of, whole), matmul(whole, cols_of)
        left = (rows_of.astype(f32) - 0.25 * row_square).astype(bf16)
        right_side = (0.25 * (cols_of.astype(f32) - col_square)).astype(bf16)
        own_square = lax.dynamic_slice_in_dim(row_square, col0, own_width, axis=1)
        inverse_root = correlation - 1.5 * offset + 0.125 * own_square + matmul(left, right_side)
    return fock, correlation, inverse_root


def solution(mesh):
    levels = mesh.shape["box"] // PAIR
    split = Mesh(mesh.devices.reshape(levels, PAIR, mesh.shape["orb"]), ("lvl", "pair", "orb"))
    in_specs = (P(BOX, None, "orb"), P(BOX, None), P(), P(BOX), P(BOX), P(BOX, None, None))
    out_specs = (P(BOX, "orb"),) * 3
    return jax.shard_map(body, mesh=split, in_specs=in_specs, out_specs=out_specs, check_vma=False)
```

profile of v0, /device:TPU:2, one launch (start us, length us, event | category | flops | bytes accessed | tf_op | source)
XLA Modules:
  0.0 188.2 jit_solution(17909687503599874703)
XLA Ops:
  1.5 0.8 copy.20.neighbours
  2.3 0.7 copy-done.11
  3.7 3.2 %pack.1 = (bf16[2,512,384]{2,1,0:T(8,128)(2,1)S(1)}, bf16[2,512,384]{2,1,0:T(8,128)(2,1)}) custom-call(s32[3]{0:T(128)S(1)} %pad_add_fusion.1.meta, s32[2,3,2]{2,1,0:T(4,128)S(1)} %copy.20.neighbours, s32[2]{0:T(128)S(1)} %copy-done.12, bf16[2,1000,384]{2,1,0:T(8,128)(2,1)} %orbitals.1, f32[2,1000]{1,0:T(2,128)S(1)} %copy-done.11), custom_call_target="tpu_custom_call" | custom-call | tf_op jit(solution)/shard_map/pack/pallas_call | solution.py:78
  6.9 1.5 collective-permute-start.1
  8.4 1.5 collective-permute-start.4
  10.5 3.6 %collective-permute-start.2 = (bf16[2,512,384]{2,1,0:T(8,128)(2,1)}, bf16[2,512,384]{2,1,0:T(8,128)(2,1)}, u32[]{:S(2)}, u32[]{:S(2)}) collective-permute-start(bf16[2,512,384]{2,1,0:T(8,128)(2,1)} %get-tuple-element.83.refs_0_), channel_id=1, source_target_pairs={{0,8},{16,24},{8,0},{24,16},{1,9},{17,25},{9,1},{25,17},{2,10},{18... | collective-permute-start | bytes 2359304 | tf_op jit(solution)/shard_map/ppermute | solution.py:24
  14.1 12.2 %collective-permute-done.1.beside_in.refs_1_ = bf16[2,512,384]{2,1,0:T(8,128)(2,1)} collective-permute-done((bf16[2,512,384]{2,1,0:T(8,128)(2,1)S(1)}, bf16[2,512,384]{2,1,0:T(8,128)(2,1)}, u32[]{:S(2)}, u32[]{:S(2)}) %collective-permute-start.1) | collective-permute-done | bytes 786464 | tf_op jit(solution)/shard_map/ppermute | solution.py:19
  26.3 1.5 collective-permute-start.6
  27.8 1.6 collective-permute-start.3
  29.4 1.6 collective-permute-start.5
  31.8 1.0 matrices.1
  35.0 9.9 %collective-permute-done.6.rest_in = bf16[2,512,384]{2,1,0:T(8,128)(2,1)S(1)} collective-permute-done((bf16[2,512,384]{2,1,0:T(8,128)(2,1)}, bf16[2,512,384]{2,1,0:T(8,128)(2,1)S(1)}, u32[]{:S(2)}, u32[]{:S(2)}) %collective-permute-start.6) | collective-permute-done | bytes 786464 | tf_op jit(solution)/shard_map/ppermute | solution.py:19
  44.9 0.9 copy-done
  45.8 1.1 copy-done.1
  47.0 2.2 %unfold.1 = (bf16[2000,384]{1,0:T(8,128)(2,1)S(1)}, bf16[1008,384]{1,0:T(8,128)(2,1)S(1)}) custom-call(s32[3]{0:T(128)S(1)} %pad_add_fusion.1.meta, bf16[2,512,384]{2,1,0:T(8,128)(2,1)} %collective-permute-done.1.beside_in.refs_1_, bf16[2,512,384]{2,1,0:T(8,128)(2,1)S(1)} %copy-done.1), custom_call_target="tpu_custom_call" | custom-call | tf_op jit(solution)/shard_map/unfold/pallas_call | solution.py:113
  49.2 0.7 slice.26
  50.7 1.6 collective-permute-start.8
  53.3 21.9 %kinetic.1 = bf16[4,1000,576]{2,1,0:T(8,128)(2,1)} custom-call(s32[2]{0:T(128)S(1)} %pad_add_fusion.2.place_meta, s32[6,2,8]{2,1,0:T(2,128)S(1)} %pad_add_fusion.facts, bf16[2,512,384]{2,1,0:T(8,128)(2,1)} %get-tuple-element.83.refs_0_, bf16[2,512,384]{2,1,0:T(8,128)(2,1)} %collective-permute-done.1.beside_in.refs_1_, ...), custom_call_target="tpu_custom_call" | custom-call | flops 20000000000 | bytes 40000000 | tf_op jit(solution)/shard_map/kinetic/pallas_call | solution.py:556
  75.9 4.8 %correlation.2.refs_6_ = f32[4,192,384]{2,1,0:T(8,128)S(1)} custom-call(s32[3]{0:T(128)S(1)} %pad_add_fusion.3.meta, bf16[2000,384]{1,0:T(8,128)(2,1)} %bitcast.5.refs_0_, bf16[2000,384]{1,0:T(8,128)(2,1)} %bitcast.6.refs_1_, bf16[2000,384]{1,0:T(8,128)(2,1)S(1)} %bitcast.36, bf16[2000,384]{1,0:T(8,128)(2,1)} %bitcast.7.refs_3_), custom_call_target="tpu_custom_call" | custom-call | flops 1179648000 | bytes 6144000 | tf_op jit(solution)/shard_map/correlation/pallas_call | solution.py:182
  80.7 4.2 %correlation.3 = bf16[4,192,384]{2,1,0:T(8,128)(2,1)S(1)} custom-call(s32[3]{0:T(128)S(1)} %pad_add_fusion.3.meta, bf16[2000,384]{1,0:T(8,128)(2,1)S(1)} %get-tuple-element.93.refs_0_, bf16[2000,384]{1,0:T(8,128)(2,1)} %collective-permute-done.9.refs_1_, bf16[1008,384]{1,0:T(8,128)(2,1)} %collective-permute-done.7.refs_2_, ...), custom_call_target="tpu_custom_call" | custom-call | flops 1179648000 | bytes 6144000 | tf_op jit(solution)/shard_map/correlation/pallas_call | solution.py:182
  84.9 6.8 %collective-permute-start.14 = (bf16[192,384]{1,0:T(8,128)(2,1)S(1)}, bf16[192,384]{1,0:T(8,128)(2,1)S(1)}, u32[]{:S(2)}, u32[]{:S(2)}) collective-permute-start(bf16[192,384]{1,0:T(8,128)(2,1)S(1)} %get-tuple-element.135), channel_id=1, source_target_pairs={{0,8},{8,0},{16,24},{24,16},{1,9},{9,1},{17,25},{25,17},{2,10},{10... | collective-permute-start | bytes 442376 | tf_op jit(solution)/shard_map/ppermute | solution.py:19
  91.8 1.7 collective-permute-start.15
  93.5 1.4 collective-permute-start.16
  94.9 8.2 %fock.2.refs_6_ = f32[4,576,384]{2,1,0:T(8,128)S(1)} custom-call(bf16[2,2000,576]{2,1,0:T(8,128)(2,1)} %bitcast.38, bf16[2000,384]{1,0:T(8,128)(2,1)} %bitcast.5.refs_0_, bf16[2000,384]{1,0:T(8,128)(2,1)} %bitcast.6.refs_1_, bf16[2000,384]{1,0:T(8,128)(2,1)S(1)} %bitcast.37, bf16[2000,384]{1,0:T(8,128)(2,1)} %bitcast.7.refs_3_), custom_call_target="tpu_custom_call" | custom-call | flops 3538944000 | bytes 6144000 | tf_op jit(solution)/shard_map/fock/pallas_call | solution.py:244
  103.0 2.7 %collective-permute-done.15.refs_2_ = bf16[192,384]{1,0:T(8,128)(2,1)S(1)} collective-permute-done((bf16[192,384]{1,0:T(8,128)(2,1)S(1)}, bf16[192,384]{1,0:T(8,128)(2,1)S(1)}, u32[]{:S(2)}, u32[]{:S(2)}) %collective-permute-start.15) | collective-permute-done | bytes 147488 | tf_op jit(solution)/shard_map/ppermute | solution.py:19
  105.7 0.8 level_sum.2
  106.5 2.6 %collective-permute-start.17 = (bf16[192,384]{1,0:T(8,128)(2,1)S(1)}, bf16[192,384]{1,0:T(8,128)(2,1)S(1)}, u32[]{:S(2)}, u32[]{:S(2)}) collective-permute-start(bf16[192,384]{1,0:T(8,128)(2,1)S(1)} %get-tuple-element.110), channel_id=1, source_target_pairs={{0,8},{8,0},{16,24},{24,16},{1,9},{9,1},{17,25},{25,17},{2,10},{10... | collective-permute-start | bytes 442376 | tf_op jit(solution)/shard_map/ppermute | solution.py:19
  109.2 1.7 collective-permute-start.18
  110.8 1.4 collective-permute-start.19
  112.2 1.2 collective-permute-start.20
  113.4 8.5 %fock.3 = (bf16[3,192,384]{2,1,0:T(8,128)(2,1)S(1)}, bf16[3,192,384]{2,1,0:T(8,128)(2,1)S(1)}, bf16[3,192,384]{2,1,0:T(8,128)(2,1)S(1)}, bf16[3,192,384]{2,1,0:T(8,128)(2,1)S(1)}) custom-call(bf16[2,2000,576]{2,1,0:T(8,128)(2,1)} %bitcast.39, bf16[2000,384]{1,0:T(8,128)(2,1)S(1)} %get-tuple-element.93.refs_0_, ...), custom_call_target="tpu_custom_call" | custom-call | flops 3538944000 | bytes 6144000 | tf_op jit(solution)/shard_map/fock/pallas_call | solution.py:244
  122.0 0.9 convert_add_fusion
  123.1 1.6 collective-permute-start.23
  124.7 1.3 collective-permute-start.21
  126.0 2.1 %collective-permute-start.25 = (bf16[3,192,384]{2,1,0:T(8,128)(2,1)S(1)}, bf16[3,192,384]{2,1,0:T(8,128)(2,1)S(1)}, u32[]{:S(2)}, u32[]{:S(2)}) collective-permute-start(bf16[3,192,384]{2,1,0:T(8,128)(2,1)S(1)} %get-tuple-element.115), channel_id=1, source_target_pairs={{0,8},{8,0},{16,24},{24,16},{1,9},{9,1},{17,25},{25,17},{2,10},{10... | collective-permute-start | bytes 1327112 | tf_op jit(solution)/shard_map/ppermute | solution.py:19
  128.1 1.2 collective-permute-start.26
  129.3 1.5 collective-permute-start.27
  130.8 0.8 collective-permute-start.24
  131.9 0.7 collective-permute-start.22
  132.7 11.8 %collective-permute-done.25.refs_1_ = bf16[3,192,384]{2,1,0:T(8,128)(2,1)S(1)} collective-permute-done((bf16[3,192,384]{2,1,0:T(8,128)(2,1)S(1)}, bf16[3,192,384]{2,1,0:T(8,128)(2,1)S(1)}, u32[]{:S(2)}, u32[]{:S(2)}) %collective-permute-start.25) | collective-permute-done | bytes 442400 | tf_op jit(solution)/shard_map/ppermute | solution.py:19
  144.4 0.8 collective-permute-start.29
  145.2 15.9 %collective-permute-done.26.refs_2_ = bf16[3,192,384]{2,1,0:T(8,128)(2,1)S(1)} collective-permute-done((bf16[3,192,384]{2,1,0:T(8,128)(2,1)S(1)}, bf16[3,192,384]{2,1,0:T(8,128)(2,1)S(1)}, u32[]{:S(2)}, u32[]{:S(2)}) %collective-permute-start.26) | collective-permute-done | bytes 442400 | tf_op jit(solution)/shard_map/ppermute | solution.py:19
  162.8 7.7 %collective-permute-done.28.refs_2_ = bf16[384,384]{1,0:T(8,128)(2,1)S(1)} collective-permute-done((bf16[384,384]{1,0:T(8,128)(2,1)S(1)}, bf16[384,384]{1,0:T(8,128)(2,1)S(1)}, u32[]{:S(2)}, u32[]{:S(2)}) %collective-permute-start.28) | collective-permute-done | bytes 294944 | tf_op jit(solution)/shard_map/ppermute | solution.py:19
  171.2 0.9 level_sum.3
  172.2 0.9 collective-permute-start.38
  173.0 7.7 %collective-permute-start.39 = (bf16[192,384]{1,0:T(8,128)(2,1)S(1)}, bf16[192,384]{1,0:T(8,128)(2,1)S(1)}, u32[]{:S(2)}, u32[]{:S(2)}) collective-permute-start(bf16[192,384]{1,0:T(8,128)(2,1)S(1)} %get-tuple-element.127), channel_id=1, source_target_pairs={{0,0},{1,8},{2,16},{3,24},{4,4},{5,12},{6,20},{7,28},{8,1},{9,9},{... | collective-permute-start | bytes 442376 | tf_op jit(solution)/shard_map/ppermute | solution.py:733
  180.7 6.4 %root.1 = f32[192,384]{1,0:T(8,128)} custom-call(s32[3]{0:T(128)S(1)} %pad_add_fusion.4.meta, bf16[384,384]{1,0:T(8,128)(2,1)S(1)} %constant_dynamic-update-slice_fusion.refs_0_, bf16[384,384]{1,0:T(8,128)(2,1)S(1)} %collective-permute-done.21.refs_1_, bf16[384,384]{1,0:T(8,128)(2,1)S(1)} %collective-permute-done.28.refs_2_, ...), custom_call_target="tpu_custom_call" | custom-call | flops 14495514624 | bytes 9437184 | tf_op jit(solution)/shard_map/root/pallas_call | solution.py:319
  187.3 0.8 maximum_add_fusion
  (104 shorter events, 10.1 us)
Async XLA Ops:
  0.6 31.1 %copy-start.7 = (bf16[112,10]{1,0:T(8,128)(2,1)S(1)}, bf16[112,10]{1,0:T(8,128)(2,1)}, u32[]{:S(2)}) copy-start(bf16[112,10]{1,0:T(8,128)(2,1)} %constant.58.clone.refs_0_) | copy-start | bytes 6724
  0.6 31.1 %copy-start.9 = (bf16[30,336]{1,0:T(8,128)(2,1)S(1)}, bf16[30,336]{1,0:T(8,128)(2,1)}, u32[]{:S(2)}) copy-start(bf16[30,336]{1,0:T(8,128)(2,1)} %constant.59.clone.refs_1_) | copy-start | bytes 60484
  0.7 31.1 %copy-start.3 = (f32[112,112]{1,0:T(8,128)S(1)}, f32[112,112]{1,0:T(8,128)}, u32[]{:S(2)}) copy-start(f32[112,112]{1,0:T(8,128)} %constant.60.clone.refs_2_) | copy-start | bytes 150532
  0.7 31.1 %copy-start.8 = (bf16[112,10]{1,0:T(8,128)(2,1)S(1)}, bf16[112,10]{1,0:T(8,128)(2,1)}, u32[]{:S(2)}) copy-start(bf16[112,10]{1,0:T(8,128)(2,1)} %constant.61.clone.refs_3_) | copy-start | bytes 6724
  0.7 31.1 %copy-start.10 = (bf16[30,336]{1,0:T(8,128)(2,1)S(1)}, bf16[30,336]{1,0:T(8,128)(2,1)}, u32[]{:S(2)}) copy-start(bf16[30,336]{1,0:T(8,128)(2,1)} %constant.62.clone.refs_4_) | copy-start | bytes 60484
  0.7 31.1 %copy-start.4 = (f32[112,112]{1,0:T(8,128)S(1)}, f32[112,112]{1,0:T(8,128)}, u32[]{:S(2)}) copy-start(f32[112,112]{1,0:T(8,128)} %constant.63.clone.refs_5_) | copy-start | bytes 150532
  0.7 31.1 %copy-start.5 = (bf16[160,10]{1,0:T(8,128)(2,1)S(1)}, bf16[160,10]{1,0:T(8,128)(2,1)}, u32[]{:S(2)}) copy-start(bf16[160,10]{1,0:T(8,128)(2,1)} %constant.64.clone.refs_6_) | copy-start | bytes 9604
  0.7 31.1 %copy-start.6 = (bf16[30,480]{1,0:T(8,128)(2,1)S(1)}, bf16[30,480]{1,0:T(8,128)(2,1)}, u32[]{:S(2)}) copy-start(bf16[30,480]{1,0:T(8,128)(2,1)} %constant.65.clone.refs_7_) | copy-start | bytes 86404
  6.9 19.4 %collective-permute-start.1 = (bf16[2,512,384]{2,1,0:T(8,128)(2,1)S(1)}, bf16[2,512,384]{2,1,0:T(8,128)(2,1)}, u32[]{:S(2)}, u32[]{:S(2)}) collective-permute-start(bf16[2,512,384]{2,1,0:T(8,128)(2,1)S(1)} %get-tuple-element.68), channel_id=1, source_target_pairs={{0,4},{4,0},{1,5},{5,1},{2,6},{6,2},{3,7},{7,3},{8,12},{12,8},{9,1... | collective-permute-start | bytes 2359304 | tf_op jit(solution)/shard_map/ppermute | solution.py:19
  8.4 21.0 %collective-permute-start.4 = (bf16[2,512,384]{2,1,0:T(8,128)(2,1)}, bf16[2,512,384]{2,1,0:T(8,128)(2,1)}, u32[]{:S(2)}, u32[]{:S(2)}) collective-permute-start(bf16[2,512,384]{2,1,0:T(8,128)(2,1)} %get-tuple-element.83.refs_0_), channel_id=1, source_target_pairs={{8,16},{16,8},{9,17},{17,9},{10,18},{18,10},{11,19},{19,11},{12,20... | collective-permute-start | bytes 2359304 | tf_op jit(solution)/shard_map/ppermute | solution.py:24
  10.0 39.2 %collective-permute-start = (bf16[2,1000,384]{2,1,0:T(8,128)(2,1)}, bf16[2,1000,384]{2,1,0:T(8,128)(2,1)S(1)}, u32[]{:S(2)}, u32[]{:S(2)}) collective-permute-start(bf16[2,1000,384]{2,1,0:T(8,128)(2,1)} %orbitals.1), channel_id=1, source_target_pairs={{0,2},{1,3},{2,0},{3,1},{4,6},{5,7},{6,4},{7,5},{8,10},{9,11},{10,... | collective-permute-start | bytes 4608008 | tf_op jit(solution)/shard_map/ppermute | solution.py:19
  10.5 23.8 %collective-permute-start.2 = (bf16[2,512,384]{2,1,0:T(8,128)(2,1)}, bf16[2,512,384]{2,1,0:T(8,128)(2,1)}, u32[]{:S(2)}, u32[]{:S(2)}) collective-permute-start(bf16[2,512,384]{2,1,0:T(8,128)(2,1)} %get-tuple-element.83.refs_0_), channel_id=1, source_target_pairs={{0,8},{16,24},{8,0},{24,16},{1,9},{17,25},{9,1},{25,17},{2,10},{18... | collective-permute-start | bytes 2359304 | tf_op jit(solution)/shard_map/ppermute | solution.py:24
  26.3 18.6 %collective-permute-start.6 = (bf16[2,512,384]{2,1,0:T(8,128)(2,1)}, bf16[2,512,384]{2,1,0:T(8,128)(2,1)S(1)}, u32[]{:S(2)}, u32[]{:S(2)}) collective-permute-start(bf16[2,512,384]{2,1,0:T(8,128)(2,1)} %get-tuple-element.83.refs_0_), channel_id=1, source_target_pairs={{0,4},{4,0},{1,5},{5,1},{2,6},{6,2},{3,7},{7,3},{8,12},{12,8},{9,1... | collective-permute-start | bytes 2359304 | tf_op jit(solution)/shard_map/ppermute | solution.py:19
  27.8 21.4 %collective-permute-start.3 = (bf16[2,512,384]{2,1,0:T(8,128)(2,1)}, bf16[2,512,384]{2,1,0:T(8,128)(2,1)}, u32[]{:S(2)}, u32[]{:S(2)}) collective-permute-start(bf16[2,512,384]{2,1,0:T(8,128)(2,1)} %collective-permute-done.1.beside_in.refs_1_), channel_id=1, source_target_pairs={{0,8},{16,24},{8,0},{24,16},{1,9},{17,25},{9,1},{25,17},{2,10},{18... | collective-permute-start | bytes 2359304 | tf_op jit(solution)/shard_map/ppermute | solution.py:24
  29.4 19.8 %collective-permute-start.5 = (bf16[2,512,384]{2,1,0:T(8,128)(2,1)}, bf16[2,512,384]{2,1,0:T(8,128)(2,1)}, u32[]{:S(2)}, u32[]{:S(2)}) collective-permute-start(bf16[2,512,384]{2,1,0:T(8,128)(2,1)} %collective-permute-done.1.beside_in.refs_1_), channel_id=1, source_target_pairs={{8,16},{16,8},{9,17},{17,9},{10,18},{18,10},{11,19},{19,11},{12,20... | collective-permute-start | bytes 2359304 | tf_op jit(solution)/shard_map/ppermute | solution.py:24
  50.6 25.3 %collective-permute-start.13 = (bf16[2,1000,384]{2,1,0:T(8,128)(2,1)S(1)}, bf16[2,1000,384]{2,1,0:T(8,128)(2,1)}, u32[]{:S(2)}, u32[]{:S(2)}) collective-permute-start(bf16[2,1000,384]{2,1,0:T(8,128)(2,1)S(1)} %collective-permute-done), channel_id=1, source_target_pairs={{0,1},{1,0},{2,3},{3,2},{4,5},{5,4},{6,7},{7,6},{8,9},{9,8},{10,11... | collective-permute-start | bytes 4608008 | tf_op jit(solution)/shard_map/ppermute | solution.py:19
  50.7 24.6 %collective-permute-start.8 = (bf16[992,384]{1,0:T(8,128)(2,1)S(1)}, bf16[992,384]{1,0:T(8,128)(2,1)}, u32[]{:S(2)}, u32[]{:S(2)}) collective-permute-start(bf16[992,384]{1,0:T(8,128)(2,1)S(1)} %slice.30), channel_id=1, source_target_pairs={{0,4},{4,0},{1,5},{5,1},{2,6},{6,2},{3,7},{7,3},{8,12},{12,8},{9,1... | collective-permute-start | bytes 2285576 | tf_op jit(solution)/shard_map/ppermute | solution.py:19
  52.2 23.0 %collective-permute-start.7 = (bf16[1008,384]{1,0:T(8,128)(2,1)S(1)}, bf16[1008,384]{1,0:T(8,128)(2,1)}, u32[]{:S(2)}, u32[]{:S(2)}) collective-permute-start(bf16[1008,384]{1,0:T(8,128)(2,1)S(1)} %get-tuple-element.78), channel_id=1, source_target_pairs={{0,2},{1,3},{2,0},{3,1},{4,6},{5,7},{6,4},{7,5},{8,10},{9,11},{10,... | collective-permute-start | bytes 2322440 | tf_op jit(solution)/shard_map/ppermute | solution.py:19
  52.8 23.1 %collective-permute-start.12 = (bf16[2,1000,384]{2,1,0:T(8,128)(2,1)}, bf16[2,1000,384]{2,1,0:T(8,128)(2,1)}, u32[]{:S(2)}, u32[]{:S(2)}) collective-permute-start(bf16[2,1000,384]{2,1,0:T(8,128)(2,1)} %orbitals.1), channel_id=1, source_target_pairs={{0,1},{1,0},{2,3},{3,2},{4,5},{5,4},{6,7},{7,6},{8,9},{9,8},{10,11... | collective-permute-start | bytes 4608008 | tf_op jit(solution)/shard_map/ppermute | solution.py:19
  52.8 27.9 %collective-permute-start.9 = (bf16[2000,384]{1,0:T(8,128)(2,1)S(1)}, bf16[2000,384]{1,0:T(8,128)(2,1)}, u32[]{:S(2)}, u32[]{:S(2)}) collective-permute-start(bf16[2000,384]{1,0:T(8,128)(2,1)S(1)} %get-tuple-element.93.refs_0_), channel_id=1, source_target_pairs={{0,1},{1,0},{2,3},{3,2},{4,5},{5,4},{6,7},{7,6},{8,9},{9,8},{10,11... | collective-permute-start | bytes 4608008 | tf_op jit(solution)/shard_map/ppermute | solution.py:19
  75.3 5.4 %collective-permute-start.10 = (bf16[1008,384]{1,0:T(8,128)(2,1)}, bf16[1008,384]{1,0:T(8,128)(2,1)}, u32[]{:S(2)}, u32[]{:S(2)}) collective-permute-start(bf16[1008,384]{1,0:T(8,128)(2,1)} %collective-permute-done.7.refs_2_), channel_id=1, source_target_pairs={{0,1},{1,0},{2,3},{3,2},{4,5},{5,4},{6,7},{7,6},{8,9},{9,8},{10,11... | collective-permute-start | bytes 2322440 | tf_op jit(solution)/shard_map/ppermute | solution.py:19
  75.3 5.3 %collective-permute-start.11 = (bf16[992,384]{1,0:T(8,128)(2,1)}, bf16[992,384]{1,0:T(8,128)(2,1)}, u32[]{:S(2)}, u32[]{:S(2)}) collective-permute-start(bf16[992,384]{1,0:T(8,128)(2,1)} %collective-permute-done.8.refs_3_), channel_id=1, source_target_pairs={{0,1},{1,0},{2,3},{3,2},{4,5},{5,4},{6,7},{7,6},{8,9},{9,8},{10,11... | collective-permute-start | bytes 2285576 | tf_op jit(solution)/shard_map/ppermute | solution.py:19
  84.9 18.1 %collective-permute-start.14 = (bf16[192,384]{1,0:T(8,128)(2,1)S(1)}, bf16[192,384]{1,0:T(8,128)(2,1)S(1)}, u32[]{:S(2)}, u32[]{:S(2)}) collective-permute-start(bf16[192,384]{1,0:T(8,128)(2,1)S(1)} %get-tuple-element.135), channel_id=1, source_target_pairs={{0,8},{8,0},{16,24},{24,16},{1,9},{9,1},{17,25},{25,17},{2,10},{10... | collective-permute-start | bytes 442376 | tf_op jit(solution)/shard_map/ppermute | solution.py:19
  91.8 14.0 %collective-permute-start.15 = (bf16[192,384]{1,0:T(8,128)(2,1)S(1)}, bf16[192,384]{1,0:T(8,128)(2,1)S(1)}, u32[]{:S(2)}, u32[]{:S(2)}) collective-permute-start(bf16[192,384]{1,0:T(8,128)(2,1)S(1)} %get-tuple-element.134), channel_id=1, source_target_pairs={{0,16},{8,24},{16,0},{24,8},{1,17},{9,25},{17,1},{25,9},{2,18},{10... | collective-permute-start | bytes 442376 | tf_op jit(solution)/shard_map/ppermute | solution.py:19
  93.5 12.2 %collective-permute-start.16 = (bf16[192,384]{1,0:T(8,128)(2,1)S(1)}, bf16[192,384]{1,0:T(8,128)(2,1)S(1)}, u32[]{:S(2)}, u32[]{:S(2)}) collective-permute-start(bf16[192,384]{1,0:T(8,128)(2,1)S(1)} %get-tuple-element.133), channel_id=1, source_target_pairs={{0,24},{8,16},{16,8},{24,0},{1,25},{9,17},{17,9},{25,1},{2,26},{10... | collective-permute-start | bytes 442376 | tf_op jit(solution)/shard_map/ppermute | solution.py:19
  106.5 16.3 %collective-permute-start.17 = (bf16[192,384]{1,0:T(8,128)(2,1)S(1)}, bf16[192,384]{1,0:T(8,128)(2,1)S(1)}, u32[]{:S(2)}, u32[]{:S(2)}) collective-permute-start(bf16[192,384]{1,0:T(8,128)(2,1)S(1)} %get-tuple-element.110), channel_id=1, source_target_pairs={{0,8},{8,0},{16,24},{24,16},{1,9},{9,1},{17,25},{25,17},{2,10},{10... | collective-permute-start | bytes 442376 | tf_op jit(solution)/shard_map/ppermute | solution.py:19
  109.2 13.9 %collective-permute-start.18 = (bf16[192,384]{1,0:T(8,128)(2,1)S(1)}, bf16[192,384]{1,0:T(8,128)(2,1)S(1)}, u32[]{:S(2)}, u32[]{:S(2)}) collective-permute-start(bf16[192,384]{1,0:T(8,128)(2,1)S(1)} %get-tuple-element.110), channel_id=1, source_target_pairs={{0,16},{8,24},{16,0},{24,8},{1,17},{9,25},{17,1},{25,9},{2,18},{10... | collective-permute-start | bytes 442376 | tf_op jit(solution)/shard_map/ppermute | solution.py:19
  110.8 12.2 %collective-permute-start.19 = (bf16[192,384]{1,0:T(8,128)(2,1)S(1)}, bf16[192,384]{1,0:T(8,128)(2,1)S(1)}, u32[]{:S(2)}, u32[]{:S(2)}) collective-permute-start(bf16[192,384]{1,0:T(8,128)(2,1)S(1)} %get-tuple-element.110), channel_id=1, source_target_pairs={{0,24},{8,16},{16,8},{24,0},{1,25},{9,17},{17,9},{25,1},{2,26},{10... | collective-permute-start | bytes 442376 | tf_op jit(solution)/shard_map/ppermute | solution.py:19
  112.2 9.7 %collective-permute-start.20 = (f32[192,192]{1,0:T(8,128)S(1)}, f32[192,192]{1,0:T(8,128)S(1)}, u32[]{:S(2)}, u32[]{:S(2)}) collective-permute-start(f32[192,192]{1,0:T(8,128)S(1)} %get-tuple-element.109), channel_id=1, source_target_pairs={{0,4},{4,0},{1,5},{5,1},{2,6},{6,2},{3,7},{7,3},{8,12},{12,8},{9,1... | collective-permute-start | bytes 442376 | tf_op jit(solution)/shard_map/ppermute | solution.py:19
  123.1 7.7 %collective-permute-start.23 = (bf16[384,384]{1,0:T(8,128)(2,1)S(1)}, bf16[384,384]{1,0:T(8,128)(2,1)S(1)}, u32[]{:S(2)}, u32[]{:S(2)}) collective-permute-start(bf16[384,384]{1,0:T(8,128)(2,1)S(1)} %constant_dynamic-update-slice_fusion.2.refs_4_), channel_id=1, source_target_pairs={{0,2},{1,3},{2,0},{3,1},{4,6},{5,7},{6,4},{7,5},{8,10},{9,11},{10,... | collective-permute-start | bytes 884744 | tf_op jit(solution)/shard_map/ppermute | solution.py:19
  124.7 7.2 %collective-permute-start.21 = (bf16[384,384]{1,0:T(8,128)(2,1)S(1)}, bf16[384,384]{1,0:T(8,128)(2,1)S(1)}, u32[]{:S(2)}, u32[]{:S(2)}) collective-permute-start(bf16[384,384]{1,0:T(8,128)(2,1)S(1)} %constant_dynamic-update-slice_fusion.refs_0_), channel_id=1, source_target_pairs={{0,4},{4,0},{1,5},{5,1},{2,6},{6,2},{3,7},{7,3},{8,12},{12,8},{9,1... | collective-permute-start | bytes 884744 | tf_op jit(solution)/shard_map/ppermute | solution.py:19
  126.0 18.4 %collective-permute-start.25 = (bf16[3,192,384]{2,1,0:T(8,128)(2,1)S(1)}, bf16[3,192,384]{2,1,0:T(8,128)(2,1)S(1)}, u32[]{:S(2)}, u32[]{:S(2)}) collective-permute-start(bf16[3,192,384]{2,1,0:T(8,128)(2,1)S(1)} %get-tuple-element.115), channel_id=1, source_target_pairs={{0,8},{8,0},{16,24},{24,16},{1,9},{9,1},{17,25},{25,17},{2,10},{10... | collective-permute-start | bytes 1327112 | tf_op jit(solution)/shard_map/ppermute | solution.py:19
  128.1 33.0 %collective-permute-start.26 = (bf16[3,192,384]{2,1,0:T(8,128)(2,1)S(1)}, bf16[3,192,384]{2,1,0:T(8,128)(2,1)S(1)}, u32[]{:S(2)}, u32[]{:S(2)}) collective-permute-start(bf16[3,192,384]{2,1,0:T(8,128)(2,1)S(1)} %get-tuple-element.116), channel_id=1, source_target_pairs={{0,16},{8,24},{16,0},{24,8},{1,17},{9,25},{17,1},{25,9},{2,18},{10... | collective-permute-start | bytes 1327112 | tf_op jit(solution)/shard_map/ppermute | solution.py:19
  129.3 31.8 %collective-permute-start.27 = (bf16[3,192,384]{2,1,0:T(8,128)(2,1)S(1)}, bf16[3,192,384]{2,1,0:T(8,128)(2,1)S(1)}, u32[]{:S(2)}, u32[]{:S(2)}) collective-permute-start(bf16[3,192,384]{2,1,0:T(8,128)(2,1)S(1)} %get-tuple-element.117), channel_id=1, source_target_pairs={{0,24},{8,16},{16,8},{24,0},{1,25},{9,17},{17,9},{25,1},{2,26},{10... | collective-permute-start | bytes 1327112 | tf_op jit(solution)/shard_map/ppermute | solution.py:19
  130.8 30.9 %collective-permute-start.24 = (bf16[384,384]{1,0:T(8,128)(2,1)S(1)}, bf16[384,384]{1,0:T(8,128)(2,1)S(1)}, u32[]{:S(2)}, u32[]{:S(2)}) collective-permute-start(bf16[384,384]{1,0:T(8,128)(2,1)S(1)} %collective-permute-done.23.refs_5_), channel_id=1, source_target_pairs={{0,4},{4,0},{1,5},{5,1},{2,6},{6,2},{3,7},{7,3},{8,12},{12,8},{9,1... | collective-permute-start | bytes 884744 | tf_op jit(solution)/shard_map/ppermute | solution.py:19
  131.9 30.0 %collective-permute-start.22 = (bf16[384,384]{1,0:T(8,128)(2,1)S(1)}, bf16[384,384]{1,0:T(8,128)(2,1)S(1)}, u32[]{:S(2)}, u32[]{:S(2)}) collective-permute-start(bf16[384,384]{1,0:T(8,128)(2,1)S(1)} %collective-permute-done.21.refs_1_), channel_id=1, source_target_pairs={{0,2},{1,3},{2,0},{3,1},{4,6},{5,7},{6,4},{7,5},{8,10},{9,11},{10,... | collective-permute-start | bytes 884744 | tf_op jit(solution)/shard_map/ppermute | solution.py:19
  144.4 17.8 %collective-permute-start.29 = (bf16[384,384]{1,0:T(8,128)(2,1)S(1)}, bf16[384,384]{1,0:T(8,128)(2,1)S(1)}, u32[]{:S(2)}, u32[]{:S(2)}) collective-permute-start(bf16[384,384]{1,0:T(8,128)(2,1)S(1)} %constant_dynamic-update-slice_fusion.2.refs_4_), channel_id=1, source_target_pairs={{0,4},{4,0},{1,5},{5,1},{2,6},{6,2},{3,7},{7,3},{8,12},{12,8},{9,1... | collective-permute-start | bytes 884744 | tf_op jit(solution)/shard_map/ppermute | solution.py:19
  161.1 1.6 collective-permute-start.34
  161.1 9.4 %collective-permute-start.28 = (bf16[384,384]{1,0:T(8,128)(2,1)S(1)}, bf16[384,384]{1,0:T(8,128)(2,1)S(1)}, u32[]{:S(2)}, u32[]{:S(2)}) collective-permute-start(bf16[384,384]{1,0:T(8,128)(2,1)S(1)} %constant_dynamic-update-slice_fusion.refs_0_), channel_id=1, source_target_pairs={{0,2},{1,3},{2,0},{3,1},{4,6},{5,7},{6,4},{7,5},{8,10},{9,11},{10,... | collective-permute-start | bytes 884744 | tf_op jit(solution)/shard_map/ppermute | solution.py:19
  161.7 8.9 %collective-permute-start.30 = (bf16[384,384]{1,0:T(8,128)(2,1)S(1)}, bf16[384,384]{1,0:T(8,128)(2,1)S(1)}, u32[]{:S(2)}, u32[]{:S(2)}) collective-permute-start(bf16[384,384]{1,0:T(8,128)(2,1)S(1)} %constant_dynamic-update-slice_fusion.refs_0_), channel_id=1, source_target_pairs={{0,1},{1,0},{2,3},{3,2},{4,5},{5,4},{6,7},{7,6},{8,9},{9,8},{10,11... | collective-permute-start | bytes 884744 | tf_op jit(solution)/shard_map/ppermute | solution.py:19
  161.9 9.2 %collective-permute-start.35 = (bf16[384,384]{1,0:T(8,128)(2,1)S(1)}, bf16[384,384]{1,0:T(8,128)(2,1)S(1)}, u32[]{:S(2)}, u32[]{:S(2)}) collective-permute-start(bf16[384,384]{1,0:T(8,128)(2,1)S(1)} %collective-permute-done.23.refs_5_), channel_id=1, source_target_pairs={{0,1},{1,0},{2,3},{3,2},{4,5},{5,4},{6,7},{7,6},{8,9},{9,8},{10,11... | collective-permute-start | bytes 884744 | tf_op jit(solution)/shard_map/ppermute | solution.py:19
  162.2 10.9 %collective-permute-start.31 = (bf16[384,384]{1,0:T(8,128)(2,1)S(1)}, bf16[384,384]{1,0:T(8,128)(2,1)S(1)}, u32[]{:S(2)}, u32[]{:S(2)}) collective-permute-start(bf16[384,384]{1,0:T(8,128)(2,1)S(1)} %collective-permute-done.21.refs_1_), channel_id=1, source_target_pairs={{0,1},{1,0},{2,3},{3,2},{4,5},{5,4},{6,7},{7,6},{8,9},{9,8},{10,11... | collective-permute-start | bytes 884744 | tf_op jit(solution)/shard_map/ppermute | solution.py:19
  162.7 9.5 %collective-permute-start.36 = (bf16[384,384]{1,0:T(8,128)(2,1)S(1)}, bf16[384,384]{1,0:T(8,128)(2,1)S(1)}, u32[]{:S(2)}, u32[]{:S(2)}) collective-permute-start(bf16[384,384]{1,0:T(8,128)(2,1)S(1)} %collective-permute-done.29.refs_6_), channel_id=1, source_target_pairs={{0,1},{1,0},{2,3},{3,2},{4,5},{5,4},{6,7},{7,6},{8,9},{9,8},{10,11... | collective-permute-start | bytes 884744 | tf_op jit(solution)/shard_map/ppermute | solution.py:19
  170.5 10.2 %collective-permute-start.32 = (bf16[384,384]{1,0:T(8,128)(2,1)S(1)}, bf16[384,384]{1,0:T(8,128)(2,1)S(1)}, u32[]{:S(2)}, u32[]{:S(2)}) collective-permute-start(bf16[384,384]{1,0:T(8,128)(2,1)S(1)} %collective-permute-done.28.refs_2_), channel_id=1, source_target_pairs={{0,1},{1,0},{2,3},{3,2},{4,5},{5,4},{6,7},{7,6},{8,9},{9,8},{10,11... | collective-permute-start | bytes 884744 | tf_op jit(solution)/shard_map/ppermute | solution.py:19
  170.5 10.2 %collective-permute-start.33 = (bf16[384,384]{1,0:T(8,128)(2,1)S(1)}, bf16[384,384]{1,0:T(8,128)(2,1)S(1)}, u32[]{:S(2)}, u32[]{:S(2)}) collective-permute-start(bf16[384,384]{1,0:T(8,128)(2,1)S(1)} %collective-permute-done.22.refs_3_), channel_id=1, source_target_pairs={{0,1},{1,0},{2,3},{3,2},{4,5},{5,4},{6,7},{7,6},{8,9},{9,8},{10,11... | collective-permute-start | bytes 884744 | tf_op jit(solution)/shard_map/ppermute | solution.py:19
  171.1 9.7 %collective-permute-start.37 = (bf16[384,384]{1,0:T(8,128)(2,1)S(1)}, bf16[384,384]{1,0:T(8,128)(2,1)S(1)}, u32[]{:S(2)}, u32[]{:S(2)}) collective-permute-start(bf16[384,384]{1,0:T(8,128)(2,1)S(1)} %collective-permute-done.24.refs_7_), channel_id=1, source_target_pairs={{0,1},{1,0},{2,3},{3,2},{4,5},{5,4},{6,7},{7,6},{8,9},{9,8},{10,11... | collective-permute-start | bytes 884744 | tf_op jit(solution)/shard_map/ppermute | solution.py:19
  172.2 15.0 %collective-permute-start.38 = (f32[192,192]{1,0:T(8,128)S(1)}, f32[192,192]{1,0:T(8,128)S(1)}, u32[]{:S(2)}, u32[]{:S(2)}) collective-permute-start(f32[192,192]{1,0:T(8,128)S(1)} %get-tuple-element.126), channel_id=1, source_target_pairs={{0,4},{4,0},{1,5},{5,1},{2,6},{6,2},{3,7},{7,3},{8,12},{12,8},{9,1... | collective-permute-start | bytes 442376 | tf_op jit(solution)/shard_map/ppermute | solution.py:19
  173.0 14.3 %collective-permute-start.39 = (bf16[192,384]{1,0:T(8,128)(2,1)S(1)}, bf16[192,384]{1,0:T(8,128)(2,1)S(1)}, u32[]{:S(2)}, u32[]{:S(2)}) collective-permute-start(bf16[192,384]{1,0:T(8,128)(2,1)S(1)} %get-tuple-element.127), channel_id=1, source_target_pairs={{0,0},{1,8},{2,16},{3,24},{4,4},{5,12},{6,20},{7,28},{8,1},{9,9},{... | collective-permute-start | bytes 442376 | tf_op jit(solution)/shard_map/ppermute | solution.py:733
  (6 other events, 62.5 us)
where the time goes:
time: 191 us; the launch traced here: 188 us
  Pallas kernels  62 us (32%)
  waiting for transfers between devices  61.1 us (32%)
  starting transfers between devices  52.4 us (27%)
  local copies, waits for them, and re-layouts  8.7 us (5%)
  other arithmetic  2.09 us (1%)
    ppermute x35, waiting for transfers between devices, swap(): return lax.ppermute(value, axis, [(i, i ^ bit) for i in range(count)])  61 us
    ppermute x35, starting transfers between devices, swap(): return lax.ppermute(value, axis, [(i, i ^ bit) for i in range(count)])  36.5 us
    pallas_call x1, Pallas kernels, kinetic(): pl.pallas_call(functools.partial(kinetic_kernel, edge, slots, levels), ou...  21.9 us
    pallas_call x2, Pallas kernels, box_fock(): pl.pallas_call(functools.partial(fock_kernel, side, counts), out_shape=ou...  16.6 us
    pallas_call x2, Pallas kernels, box_correlation(): pl.pallas_call(functools.partial(correlation_kernel, share, counts), out_...  8.95 us
    ppermute x4, starting transfers between devices, trade(): return lax.ppermute(value, axis, pairs + [(b, a) for a, b in pairs])  8.27 us
    ppermute x1, starting transfers between devices, body(): got = (swap(other, 'pair', 1), lax.ppermute(share, BOX + ('orb',), to))  7.66 us
    pallas_call x1, Pallas kernels, root_of(): pl.pallas_call(functools.partial(root_kernel, levels), out_shape=jax.Shap...  6.38 us
  transfers between devices with their start and end apart: 40, of which 10 were waited for; matrix products, arithmetic and copies ran while one was open for 2% of the time, Pallas kernels for 29%

commit v1 on v0

--- a/solution.py
+++ b/solution.py
@@ -80,7 +80,7 @@
         out_shape=[jax.ShapeDtypeStruct((slots, padded, width), bf16)] * 2,
         in_specs=[smem, smem, smem, vmem, vmem],
         out_specs=[vmem, vmem],
-        compiler_params=params(24),
+        compiler_params=params(8),
         name="pack",
     )(meta, neighbours, levels, orbitals, pot)
 
@@ -116,14 +116,14 @@
             jax.ShapeDtypeStruct((2 * slots * fold, width), bf16),
             jax.ShapeDtypeStruct((cut, width), bf16),
         ],
-        in_specs=[pl.BlockSpec(memory_space=pltpu.SMEM)] + [pl.BlockSpec(memory_space=pltpu.HBM)] * 2,
+        in_specs=[pl.BlockSpec(memory_space=pltpu.SMEM)] + [pl.BlockSpec(memory_space=pl.ANY)] * 2,
         out_specs=[vmem, vmem],
         scratch_shapes=[
             pltpu.VMEM(beside.shape, bf16),
             pltpu.VMEM(beside.shape, bf16),
             pltpu.SemaphoreType.DMA((2,)),
         ],
-        compiler_params=params(24),
+        compiler_params=params(8),
         name="unfold",
     )(meta, beside, rest)
 
@@ -540,7 +540,7 @@
         out_shape=[jax.ShapeDtypeStruct(shape, bf16) for shape in shapes],
         in_specs=[vmem] * 11,
         out_specs=[vmem] * 5,
-        compiler_params=params(24),
+        compiler_params=params(8),
         name="matrices",
     )(stacked, deriv_blocks, *constants)
 
@@ -611,7 +611,7 @@
         out_shape=[jax.ShapeDtypeStruct((tall, width), bf16), turned, turned],
         in_specs=[pl.BlockSpec(memory_space=pltpu.SMEM)] + [vmem] * len(blocks),
         out_specs=[vmem] * 3,
-        compiler_params=params(24),
+        compiler_params=params(8),
         name="level_sum",
     )(meta, *blocks)
 
@@ -716,9 +716,10 @@
         top, low = join(pieces[: level_count // 2]), join(pieces[level_count // 2 :])
         sent = [fock_blocks[0]] + [swap(fock_blocks[step], "lvl", step) for step in range(1, level_count)]
         got = [swap(top, "pair", 1), swap(low, "orb", 2)]
+        got, sent[:2] = lax.optimization_barrier((got, sent[:2]))
         tops, lows = [top, got[0]], [low, got[1]]
         far_tops, far_lows = [swap(piece, "orb", 2) for piece in tops], [swap(piece, "pair", 1) for piece in lows]
-        far_tops[1], far_lows[1], sent = lax.optimization_barrier((far_tops[1], far_lows[1], sent))
+        far_tops, far_lows, sent = lax.optimization_barrier((far_tops, far_lows, sent))
         pieces = tops + far_tops + lows + far_lows
         pieces += [swap(piece, "orb", 1) for piece in pieces]
         root_meta = jnp.stack([level, pair, orb]).astype(jnp.int32)

time: 191 us -> 182 us (0.953)
  waiting for transfers between devices: 61.1 us -> 53 us
  Pallas kernels: 62 us -> 65.3 us
  starting transfers between devices: 52.4 us -> 49.4 us
    ppermute x35, waiting for transfers between devices: 61 us -> 53 us  [swap(): return lax.ppermute(value, axis, [(i, i ^ bit) for i in range(count)])]
    pallas_call x1, Pallas kernels: 21.9 us -> 25.3 us  [kinetic(): pl.pallas_call(functools.partial(kinetic_kernel, edge, slots, levels), ou...]
    ppermute x35, starting transfers between devices: 36.5 us -> 33.2 us  [swap(): return lax.ppermute(value, axis, [(i, i ^ bit) for i in range(count)])]
  transfers between devices with their start and end apart: 40 -> 40, of which waited for: 10 -> 9; matrix products, arithmetic and copies ran while one was open for 2% -> 2% of each run, Pallas kernels for 29% -> 32%
where the time goes in v1:
time: 182 us; the launch traced here: 180 us
  Pallas kernels  65.3 us (36%)
  waiting for transfers between devices  53 us (29%)
  starting transfers between devices  49.4 us (27%)
  local copies, waits for them, and re-layouts  8.7 us (5%)
  other arithmetic  2.1 us (1%)
  between operations  1.82 us (1%)
    ppermute x35, waiting for transfers between devices, swap(): return lax.ppermute(value, axis, [(i, i ^ bit) for i in range(count)])  53 us
    ppermute x35, starting transfers between devices, swap(): return lax.ppermute(value, axis, [(i, i ^ bit) for i in range(count)])  33.2 us
    pallas_call x1, Pallas kernels, kinetic(): pl.pallas_call(functools.partial(kinetic_kernel, edge, slots, levels), ou...  25.3 us
    pallas_call x2, Pallas kernels, box_fock(): pl.pallas_call(functools.partial(fock_kernel, side, counts), out_shape=ou...  16.6 us
    pallas_call x2, Pallas kernels, box_correlation(): pl.pallas_call(functools.partial(correlation_kernel, share, counts), out_...  8.96 us
    ppermute x4, starting transfers between devices, trade(): return lax.ppermute(value, axis, pairs + [(b, a) for a, b in pairs])  8.27 us
    ppermute x1, starting transfers between devices, body(): got = (swap(other, 'pair', 1), lax.ppermute(share, BOX + ('orb',), to))  7.95 us
    pallas_call x1, Pallas kernels, root_of(): pl.pallas_call(functools.partial(root_kernel, levels), out_shape=jax.Shap...  6.38 us
  transfers between devices with their start and end apart: 40, of which 9 were waited for; matrix products, arithmetic and copies ran while one was open for 2% of the time, Pallas kernels for 32%

profile of v1, /device:TPU:2, one launch (start us, length us, event | category | flops | bytes accessed | tf_op | source)
XLA Modules:
  0.0 180.4 jit_solution(5288119142151259617)
XLA Ops:
  1.5 0.8 copy.20.neighbours
  2.3 0.7 copy-done.11
  3.7 3.2 %pack.1 = (bf16[2,512,384]{2,1,0:T(8,128)(2,1)S(1)}, bf16[2,512,384]{2,1,0:T(8,128)(2,1)}) custom-call(s32[3]{0:T(128)S(1)} %pad_add_fusion.1.meta, s32[2,3,2]{2,1,0:T(4,128)S(1)} %copy.20.neighbours, s32[2]{0:T(128)S(1)} %copy-done.12, bf16[2,1000,384]{2,1,0:T(8,128)(2,1)} %orbitals.1, f32[2,1000]{1,0:T(2,128)S(1)} %copy-done.11), custom_call_target="tpu_custom_call" | custom-call | tf_op jit(solution)/shard_map/pack/pallas_call | solution.py:78
  6.9 1.5 collective-permute-start.1
  8.4 1.5 collective-permute-start.4
  10.5 3.6 %collective-permute-start.2 = (bf16[2,512,384]{2,1,0:T(8,128)(2,1)}, bf16[2,512,384]{2,1,0:T(8,128)(2,1)}, u32[]{:S(2)}, u32[]{:S(2)}) collective-permute-start(bf16[2,512,384]{2,1,0:T(8,128)(2,1)} %get-tuple-element.89.refs_0_), channel_id=1, source_target_pairs={{0,8},{16,24},{8,0},{24,16},{1,9},{17,25},{9,1},{25,17},{2,10},{18... | collective-permute-start | bytes 2359304 | tf_op jit(solution)/shard_map/ppermute | solution.py:24
  14.1 12.2 %collective-permute-done.1.beside_in.refs_1_ = bf16[2,512,384]{2,1,0:T(8,128)(2,1)} collective-permute-done((bf16[2,512,384]{2,1,0:T(8,128)(2,1)S(1)}, bf16[2,512,384]{2,1,0:T(8,128)(2,1)}, u32[]{:S(2)}, u32[]{:S(2)}) %collective-permute-start.1) | collective-permute-done | bytes 786464 | tf_op jit(solution)/shard_map/ppermute | solution.py:19
  26.3 1.5 collective-permute-start.6
  27.8 1.6 collective-permute-start.3
  29.4 1.6 collective-permute-start.5
  31.0 0.7 slice.21
  31.8 1.0 matrices.1
  33.0 0.7 slice.22
  33.6 0.7 slice.29
  34.3 0.7 slice.28
  35.0 9.9 %collective-permute-done.6.rest_in = bf16[2,512,384]{2,1,0:T(8,128)(2,1)S(1)} collective-permute-done((bf16[2,512,384]{2,1,0:T(8,128)(2,1)}, bf16[2,512,384]{2,1,0:T(8,128)(2,1)S(1)}, u32[]{:S(2)}, u32[]{:S(2)}) %collective-permute-start.6) | collective-permute-done | bytes 786464 | tf_op jit(solution)/shard_map/ppermute | solution.py:19
  44.9 0.9 copy-done
  45.8 1.1 copy-done.1
  47.0 2.2 %unfold.1 = (bf16[2000,384]{1,0:T(8,128)(2,1)S(1)}, bf16[1008,384]{1,0:T(8,128)(2,1)S(1)}) custom-call(s32[3]{0:T(128)S(1)} %pad_add_fusion.1.meta, bf16[2,512,384]{2,1,0:T(8,128)(2,1)} %collective-permute-done.1.beside_in.refs_1_, bf16[2,512,384]{2,1,0:T(8,128)(2,1)S(1)} %copy-done.1), custom_call_target="tpu_custom_call" | custom-call | tf_op jit(solution)/shard_map/unfold/pallas_call | solution.py:113
  49.2 0.7 slice.26
  49.9 0.7 slice.27
  50.7 1.6 collective-permute-start.8
  53.3 25.3 %kinetic.1 = bf16[4,1000,576]{2,1,0:T(8,128)(2,1)} custom-call(s32[2]{0:T(128)S(1)} %pad_add_fusion.2.place_meta, s32[6,2,8]{2,1,0:T(2,128)S(1)} %pad_add_fusion.facts, bf16[2,512,384]{2,1,0:T(8,128)(2,1)} %get-tuple-element.89.refs_0_, bf16[2,512,384]{2,1,0:T(8,128)(2,1)} %collective-permute-done.1.beside_in.refs_1_, ...), custom_call_target="tpu_custom_call" | custom-call | flops 20000000000 | bytes 40000000 | tf_op jit(solution)/shard_map/kinetic/pallas_call | solution.py:556
  79.2 4.8 %correlation.2.refs_6_ = f32[4,192,384]{2,1,0:T(8,128)S(1)} custom-call(s32[3]{0:T(128)S(1)} %pad_add_fusion.3.meta, bf16[2000,384]{1,0:T(8,128)(2,1)} %bitcast.5.refs_0_, bf16[2000,384]{1,0:T(8,128)(2,1)} %bitcast.6.refs_1_, bf16[2000,384]{1,0:T(8,128)(2,1)S(1)} %bitcast.36, bf16[2000,384]{1,0:T(8,128)(2,1)} %bitcast.7.refs_3_), custom_call_target="tpu_custom_call" | custom-call | flops 1179648000 | bytes 6144000 | tf_op jit(solution)/shard_map/correlation/pallas_call | solution.py:182
  84.1 4.2 %correlation.3 = bf16[4,192,384]{2,1,0:T(8,128)(2,1)S(1)} custom-call(s32[3]{0:T(128)S(1)} %pad_add_fusion.3.meta, bf16[2000,384]{1,0:T(8,128)(2,1)S(1)} %get-tuple-element.99.refs_0_, bf16[2000,384]{1,0:T(8,128)(2,1)} %collective-permute-done.9.refs_1_, bf16[1008,384]{1,0:T(8,128)(2,1)} %collective-permute-done.7.refs_2_, ...), custom_call_target="tpu_custom_call" | custom-call | flops 1179648000 | bytes 6144000 | tf_op jit(solution)/shard_map/correlation/pallas_call | solution.py:182
  88.3 3.5 %collective-permute-start.14 = (bf16[192,384]{1,0:T(8,128)(2,1)S(1)}, bf16[192,384]{1,0:T(8,128)(2,1)S(1)}, u32[]{:S(2)}, u32[]{:S(2)}) collective-permute-start(bf16[192,384]{1,0:T(8,128)(2,1)S(1)} %get-tuple-element.147), channel_id=1, source_target_pairs={{0,8},{8,0},{16,24},{24,16},{1,9},{9,1},{17,25},{25,17},{2,10},{10... | collective-permute-start | bytes 442376 | tf_op jit(solution)/shard_map/ppermute | solution.py:19
  91.8 2.4 %collective-permute-start.16 = (bf16[192,384]{1,0:T(8,128)(2,1)S(1)}, bf16[192,384]{1,0:T(8,128)(2,1)S(1)}, u32[]{:S(2)}, u32[]{:S(2)}) collective-permute-start(bf16[192,384]{1,0:T(8,128)(2,1)S(1)} %get-tuple-element.145), channel_id=1, source_target_pairs={{0,24},{8,16},{16,8},{24,0},{1,25},{9,17},{17,9},{25,1},{2,26},{10... | collective-permute-start | bytes 442376 | tf_op jit(solution)/shard_map/ppermute | solution.py:19
  94.3 8.2 %fock.2.refs_6_ = f32[4,576,384]{2,1,0:T(8,128)S(1)} custom-call(bf16[2,2000,576]{2,1,0:T(8,128)(2,1)} %bitcast.38, bf16[2000,384]{1,0:T(8,128)(2,1)} %bitcast.5.refs_0_, bf16[2000,384]{1,0:T(8,128)(2,1)} %bitcast.6.refs_1_, bf16[2000,384]{1,0:T(8,128)(2,1)S(1)} %bitcast.37, bf16[2000,384]{1,0:T(8,128)(2,1)} %bitcast.7.refs_3_), custom_call_target="tpu_custom_call" | custom-call | flops 3538944000 | bytes 6144000 | tf_op jit(solution)/shard_map/fock/pallas_call | solution.py:244
  102.5 2.5 %collective-permute-done.15.refs_2_ = bf16[192,384]{1,0:T(8,128)(2,1)S(1)} collective-permute-done((bf16[192,384]{1,0:T(8,128)(2,1)S(1)}, bf16[192,384]{1,0:T(8,128)(2,1)S(1)}, u32[]{:S(2)}, u32[]{:S(2)}) %collective-permute-start.15) | collective-permute-done | bytes 147488 | tf_op jit(solution)/shard_map/ppermute | solution.py:19
  104.9 0.8 level_sum.2
  105.7 3.4 %collective-permute-start.17 = (bf16[192,384]{1,0:T(8,128)(2,1)S(1)}, bf16[192,384]{1,0:T(8,128)(2,1)S(1)}, u32[]{:S(2)}, u32[]{:S(2)}) collective-permute-start(bf16[192,384]{1,0:T(8,128)(2,1)S(1)} %get-tuple-element.116), channel_id=1, source_target_pairs={{0,8},{8,0},{16,24},{24,16},{1,9},{9,1},{17,25},{25,17},{2,10},{10... | collective-permute-start | bytes 442376 | tf_op jit(solution)/shard_map/ppermute | solution.py:19
  109.1 2.4 %collective-permute-start.19 = (bf16[192,384]{1,0:T(8,128)(2,1)S(1)}, bf16[192,384]{1,0:T(8,128)(2,1)S(1)}, u32[]{:S(2)}, u32[]{:S(2)}) collective-permute-start(bf16[192,384]{1,0:T(8,128)(2,1)S(1)} %get-tuple-element.116), channel_id=1, source_target_pairs={{0,24},{8,16},{16,8},{24,0},{1,25},{9,17},{17,9},{25,1},{2,26},{10... | collective-permute-start | bytes 442376 | tf_op jit(solution)/shard_map/ppermute | solution.py:19
  111.6 1.2 collective-permute-start.20
  112.8 8.5 %fock.3 = (bf16[3,192,384]{2,1,0:T(8,128)(2,1)S(1)}, bf16[3,192,384]{2,1,0:T(8,128)(2,1)S(1)}, bf16[3,192,384]{2,1,0:T(8,128)(2,1)S(1)}, bf16[3,192,384]{2,1,0:T(8,128)(2,1)S(1)}) custom-call(bf16[2,2000,576]{2,1,0:T(8,128)(2,1)} %bitcast.39, bf16[2000,384]{1,0:T(8,128)(2,1)S(1)} %get-tuple-element.99.refs_0_, ...), custom_call_target="tpu_custom_call" | custom-call | flops 3538944000 | bytes 6144000 | tf_op jit(solution)/shard_map/fock/pallas_call | solution.py:244
  121.3 0.9 convert_add_fusion
  122.3 1.6 collective-permute-start.23
  123.9 1.3 collective-permute-start.22
  125.2 2.9 %collective-permute-start.24 = (bf16[3,192,384]{2,1,0:T(8,128)(2,1)S(1)}, bf16[3,192,384]{2,1,0:T(8,128)(2,1)S(1)}, u32[]{:S(2)}, u32[]{:S(2)}) collective-permute-start(bf16[3,192,384]{2,1,0:T(8,128)(2,1)S(1)} %get-tuple-element.121), channel_id=1, source_target_pairs={{0,8},{8,0},{16,24},{24,16},{1,9},{9,1},{17,25},{25,17},{2,10},{10... | collective-permute-start | bytes 1327112 | tf_op jit(solution)/shard_map/ppermute | solution.py:19
  128.2 2.4 %collective-permute-start.29 = (bf16[3,192,384]{2,1,0:T(8,128)(2,1)S(1)}, bf16[3,192,384]{2,1,0:T(8,128)(2,1)S(1)}, u32[]{:S(2)}, u32[]{:S(2)}) collective-permute-start(bf16[3,192,384]{2,1,0:T(8,128)(2,1)S(1)} %get-tuple-element.127), channel_id=1, source_target_pairs={{0,24},{8,16},{16,8},{24,0},{1,25},{9,17},{17,9},{25,1},{2,26},{10... | collective-permute-start | bytes 1327112 | tf_op jit(solution)/shard_map/ppermute | solution.py:19
  130.5 0.8 collective-permute-start.26
  131.6 0.9 collective-permute-start.21
  132.5 11.8 %collective-permute-done.24.refs_1_ = bf16[3,192,384]{2,1,0:T(8,128)(2,1)S(1)} collective-permute-done((bf16[3,192,384]{2,1,0:T(8,128)(2,1)S(1)}, bf16[3,192,384]{2,1,0:T(8,128)(2,1)S(1)}, u32[]{:S(2)}, u32[]{:S(2)}) %collective-permute-start.24) | collective-permute-done | bytes 442400 | tf_op jit(solution)/shard_map/ppermute | solution.py:19
  145.7 15.5 %collective-permute-done.28.refs_2_ = bf16[3,192,384]{2,1,0:T(8,128)(2,1)S(1)} collective-permute-done((bf16[3,192,384]{2,1,0:T(8,128)(2,1)S(1)}, bf16[3,192,384]{2,1,0:T(8,128)(2,1)S(1)}, u32[]{:S(2)}, u32[]{:S(2)}) %collective-permute-start.28) | collective-permute-done | bytes 442400 | tf_op jit(solution)/shard_map/ppermute | solution.py:19
  163.3 0.9 level_sum.3
  164.3 0.8 collective-permute-start.38
  165.1 7.9 %collective-permute-start.39 = (bf16[192,384]{1,0:T(8,128)(2,1)S(1)}, bf16[192,384]{1,0:T(8,128)(2,1)S(1)}, u32[]{:S(2)}, u32[]{:S(2)}) collective-permute-start(bf16[192,384]{1,0:T(8,128)(2,1)S(1)} %get-tuple-element.139), channel_id=1, source_target_pairs={{0,0},{1,8},{2,16},{3,24},{4,4},{5,12},{6,20},{7,28},{8,1},{9,9},{... | collective-permute-start | bytes 442376 | tf_op jit(solution)/shard_map/ppermute | solution.py:734
  173.1 6.4 %root.1 = f32[192,384]{1,0:T(8,128)} custom-call(s32[3]{0:T(128)S(1)} %pad_add_fusion.4.meta, bf16[384,384]{1,0:T(8,128)(2,1)S(1)} %constant_dynamic-update-slice_fusion.refs_0_, bf16[384,384]{1,0:T(8,128)(2,1)S(1)} %collective-permute-done.22.refs_1_, bf16[384,384]{1,0:T(8,128)(2,1)S(1)} %collective-permute-done.21.refs_2_, ...), custom_call_target="tpu_custom_call" | custom-call | flops 14495514624 | bytes 9437184 | tf_op jit(solution)/shard_map/root/pallas_call | solution.py:319
  179.6 0.8 maximum_add_fusion
  (104 shorter events, 7.5 us)
Async XLA Ops:
  0.6 31.1 %copy-start.7 = (bf16[112,10]{1,0:T(8,128)(2,1)S(1)}, bf16[112,10]{1,0:T(8,128)(2,1)}, u32[]{:S(2)}) copy-start(bf16[112,10]{1,0:T(8,128)(2,1)} %constant.58.clone.refs_0_) | copy-start | bytes 6724
  0.6 31.1 %copy-start.9 = (bf16[30,336]{1,0:T(8,128)(2,1)S(1)}, bf16[30,336]{1,0:T(8,128)(2,1)}, u32[]{:S(2)}) copy-start(bf16[30,336]{1,0:T(8,128)(2,1)} %constant.59.clone.refs_1_) | copy-start | bytes 60484
  0.7 31.1 %copy-start.3 = (f32[112,112]{1,0:T(8,128)S(1)}, f32[112,112]{1,0:T(8,128)}, u32[]{:S(2)}) copy-start(f32[112,112]{1,0:T(8,128)} %constant.60.clone.refs_2_) | copy-start | bytes 150532
  0.7 31.1 %copy-start.8 = (bf16[112,10]{1,0:T(8,128)(2,1)S(1)}, bf16[112,10]{1,0:T(8,128)(2,1)}, u32[]{:S(2)}) copy-start(bf16[112,10]{1,0:T(8,128)(2,1)} %constant.61.clone.refs_3_) | copy-start | bytes 6724
  0.7 31.1 %copy-start.10 = (bf16[30,336]{1,0:T(8,128)(2,1)S(1)}, bf16[30,336]{1,0:T(8,128)(2,1)}, u32[]{:S(2)}) copy-start(bf16[30,336]{1,0:T(8,128)(2,1)} %constant.62.clone.refs_4_) | copy-start | bytes 60484
  0.7 31.1 %copy-start.4 = (f32[112,112]{1,0:T(8,128)S(1)}, f32[112,112]{1,0:T(8,128)}, u32[]{:S(2)}) copy-start(f32[112,112]{1,0:T(8,128)} %constant.63.clone.refs_5_) | copy-start | bytes 150532
  0.7 31.1 %copy-start.5 = (bf16[160,10]{1,0:T(8,128)(2,1)S(1)}, bf16[160,10]{1,0:T(8,128)(2,1)}, u32[]{:S(2)}) copy-start(bf16[160,10]{1,0:T(8,128)(2,1)} %constant.64.clone.refs_6_) | copy-start | bytes 9604
  0.7 31.1 %copy-start.6 = (bf16[30,480]{1,0:T(8,128)(2,1)S(1)}, bf16[30,480]{1,0:T(8,128)(2,1)}, u32[]{:S(2)}) copy-start(bf16[30,480]{1,0:T(8,128)(2,1)} %constant.65.clone.refs_7_) | copy-start | bytes 86404
  6.9 19.4 %collective-permute-start.1 = (bf16[2,512,384]{2,1,0:T(8,128)(2,1)S(1)}, bf16[2,512,384]{2,1,0:T(8,128)(2,1)}, u32[]{:S(2)}, u32[]{:S(2)}) collective-permute-start(bf16[2,512,384]{2,1,0:T(8,128)(2,1)S(1)} %get-tuple-element.74), channel_id=1, source_target_pairs={{0,4},{4,0},{1,5},{5,1},{2,6},{6,2},{3,7},{7,3},{8,12},{12,8},{9,1... | collective-permute-start | bytes 2359304 | tf_op jit(solution)/shard_map/ppermute | solution.py:19
  8.4 21.0 %collective-permute-start.4 = (bf16[2,512,384]{2,1,0:T(8,128)(2,1)}, bf16[2,512,384]{2,1,0:T(8,128)(2,1)}, u32[]{:S(2)}, u32[]{:S(2)}) collective-permute-start(bf16[2,512,384]{2,1,0:T(8,128)(2,1)} %get-tuple-element.89.refs_0_), channel_id=1, source_target_pairs={{8,16},{16,8},{9,17},{17,9},{10,18},{18,10},{11,19},{19,11},{12,20... | collective-permute-start | bytes 2359304 | tf_op jit(solution)/shard_map/ppermute | solution.py:24
  10.0 39.2 %collective-permute-start = (bf16[2,1000,384]{2,1,0:T(8,128)(2,1)}, bf16[2,1000,384]{2,1,0:T(8,128)(2,1)S(1)}, u32[]{:S(2)}, u32[]{:S(2)}) collective-permute-start(bf16[2,1000,384]{2,1,0:T(8,128)(2,1)} %orbitals.1), channel_id=1, source_target_pairs={{0,2},{1,3},{2,0},{3,1},{4,6},{5,7},{6,4},{7,5},{8,10},{9,11},{10,... | collective-permute-start | bytes 4608008 | tf_op jit(solution)/shard_map/ppermute | solution.py:19
  10.5 23.8 %collective-permute-start.2 = (bf16[2,512,384]{2,1,0:T(8,128)(2,1)}, bf16[2,512,384]{2,1,0:T(8,128)(2,1)}, u32[]{:S(2)}, u32[]{:S(2)}) collective-permute-start(bf16[2,512,384]{2,1,0:T(8,128)(2,1)} %get-tuple-element.89.refs_0_), channel_id=1, source_target_pairs={{0,8},{16,24},{8,0},{24,16},{1,9},{17,25},{9,1},{25,17},{2,10},{18... | collective-permute-start | bytes 2359304 | tf_op jit(solution)/shard_map/ppermute | solution.py:24
  26.3 18.6 %collective-permute-start.6 = (bf16[2,512,384]{2,1,0:T(8,128)(2,1)}, bf16[2,512,384]{2,1,0:T(8,128)(2,1)S(1)}, u32[]{:S(2)}, u32[]{:S(2)}) collective-permute-start(bf16[2,512,384]{2,1,0:T(8,128)(2,1)} %get-tuple-element.89.refs_0_), channel_id=1, source_target_pairs={{0,4},{4,0},{1,5},{5,1},{2,6},{6,2},{3,7},{7,3},{8,12},{12,8},{9,1... | collective-permute-start | bytes 2359304 | tf_op jit(solution)/shard_map/ppermute | solution.py:19
  27.8 21.4 %collective-permute-start.3 = (bf16[2,512,384]{2,1,0:T(8,128)(2,1)}, bf16[2,512,384]{2,1,0:T(8,128)(2,1)}, u32[]{:S(2)}, u32[]{:S(2)}) collective-permute-start(bf16[2,512,384]{2,1,0:T(8,128)(2,1)} %collective-permute-done.1.beside_in.refs_1_), channel_id=1, source_target_pairs={{0,8},{16,24},{8,0},{24,16},{1,9},{17,25},{9,1},{25,17},{2,10},{18... | collective-permute-start | bytes 2359304 | tf_op jit(solution)/shard_map/ppermute | solution.py:24
  29.4 19.8 %collective-permute-start.5 = (bf16[2,512,384]{2,1,0:T(8,128)(2,1)}, bf16[2,512,384]{2,1,0:T(8,128)(2,1)}, u32[]{:S(2)}, u32[]{:S(2)}) collective-permute-start(bf16[2,512,384]{2,1,0:T(8,128)(2,1)} %collective-permute-done.1.beside_in.refs_1_), channel_id=1, source_target_pairs={{8,16},{16,8},{9,17},{17,9},{10,18},{18,10},{11,19},{19,11},{12,20... | collective-permute-start | bytes 2359304 | tf_op jit(solution)/shard_map/ppermute | solution.py:24
  50.6 28.6 %collective-permute-start.13 = (bf16[2,1000,384]{2,1,0:T(8,128)(2,1)S(1)}, bf16[2,1000,384]{2,1,0:T(8,128)(2,1)}, u32[]{:S(2)}, u32[]{:S(2)}) collective-permute-start(bf16[2,1000,384]{2,1,0:T(8,128)(2,1)S(1)} %collective-permute-done), channel_id=1, source_target_pairs={{0,1},{1,0},{2,3},{3,2},{4,5},{5,4},{6,7},{7,6},{8,9},{9,8},{10,11... | collective-permute-start | bytes 4608008 | tf_op jit(solution)/shard_map/ppermute | solution.py:19
  50.7 27.9 %collective-permute-start.8 = (bf16[992,384]{1,0:T(8,128)(2,1)S(1)}, bf16[992,384]{1,0:T(8,128)(2,1)}, u32[]{:S(2)}, u32[]{:S(2)}) collective-permute-start(bf16[992,384]{1,0:T(8,128)(2,1)S(1)} %slice.30), channel_id=1, source_target_pairs={{0,4},{4,0},{1,5},{5,1},{2,6},{6,2},{3,7},{7,3},{8,12},{12,8},{9,1... | collective-permute-start | bytes 2285576 | tf_op jit(solution)/shard_map/ppermute | solution.py:19
  52.2 26.4 %collective-permute-start.7 = (bf16[1008,384]{1,0:T(8,128)(2,1)S(1)}, bf16[1008,384]{1,0:T(8,128)(2,1)}, u32[]{:S(2)}, u32[]{:S(2)}) collective-permute-start(bf16[1008,384]{1,0:T(8,128)(2,1)S(1)} %get-tuple-element.84), channel_id=1, source_target_pairs={{0,2},{1,3},{2,0},{3,1},{4,6},{5,7},{6,4},{7,5},{8,10},{9,11},{10,... | collective-permute-start | bytes 2322440 | tf_op jit(solution)/shard_map/ppermute | solution.py:19
  52.8 26.4 %collective-permute-start.12 = (bf16[2,1000,384]{2,1,0:T(8,128)(2,1)}, bf16[2,1000,384]{2,1,0:T(8,128)(2,1)}, u32[]{:S(2)}, u32[]{:S(2)}) collective-permute-start(bf16[2,1000,384]{2,1,0:T(8,128)(2,1)} %orbitals.1), channel_id=1, source_target_pairs={{0,1},{1,0},{2,3},{3,2},{4,5},{5,4},{6,7},{7,6},{8,9},{9,8},{10,11... | collective-permute-start | bytes 4608008 | tf_op jit(solution)/shard_map/ppermute | solution.py:19
  52.8 31.3 %collective-permute-start.9 = (bf16[2000,384]{1,0:T(8,128)(2,1)S(1)}, bf16[2000,384]{1,0:T(8,128)(2,1)}, u32[]{:S(2)}, u32[]{:S(2)}) collective-permute-start(bf16[2000,384]{1,0:T(8,128)(2,1)S(1)} %get-tuple-element.99.refs_0_), channel_id=1, source_target_pairs={{0,1},{1,0},{2,3},{3,2},{4,5},{5,4},{6,7},{7,6},{8,9},{9,8},{10,11... | collective-permute-start | bytes 4608008 | tf_op jit(solution)/shard_map/ppermute | solution.py:19
  78.6 5.4 %collective-permute-start.10 = (bf16[1008,384]{1,0:T(8,128)(2,1)}, bf16[1008,384]{1,0:T(8,128)(2,1)}, u32[]{:S(2)}, u32[]{:S(2)}) collective-permute-start(bf16[1008,384]{1,0:T(8,128)(2,1)} %collective-permute-done.7.refs_2_), channel_id=1, source_target_pairs={{0,1},{1,0},{2,3},{3,2},{4,5},{5,4},{6,7},{7,6},{8,9},{9,8},{10,11... | collective-permute-start | bytes 2322440 | tf_op jit(solution)/shard_map/ppermute | solution.py:19
  78.7 5.3 %collective-permute-start.11 = (bf16[992,384]{1,0:T(8,128)(2,1)}, bf16[992,384]{1,0:T(8,128)(2,1)}, u32[]{:S(2)}, u32[]{:S(2)}) collective-permute-start(bf16[992,384]{1,0:T(8,128)(2,1)} %collective-permute-done.8.refs_3_), channel_id=1, source_target_pairs={{0,1},{1,0},{2,3},{3,2},{4,5},{5,4},{6,7},{7,6},{8,9},{9,8},{10,11... | collective-permute-start | bytes 2285576 | tf_op jit(solution)/shard_map/ppermute | solution.py:19
  88.3 14.2 %collective-permute-start.14 = (bf16[192,384]{1,0:T(8,128)(2,1)S(1)}, bf16[192,384]{1,0:T(8,128)(2,1)S(1)}, u32[]{:S(2)}, u32[]{:S(2)}) collective-permute-start(bf16[192,384]{1,0:T(8,128)(2,1)S(1)} %get-tuple-element.147), channel_id=1, source_target_pairs={{0,8},{8,0},{16,24},{24,16},{1,9},{9,1},{17,25},{25,17},{2,10},{10... | collective-permute-start | bytes 442376 | tf_op jit(solution)/shard_map/ppermute | solution.py:19
  91.8 13.1 %collective-permute-start.15 = (bf16[192,384]{1,0:T(8,128)(2,1)S(1)}, bf16[192,384]{1,0:T(8,128)(2,1)S(1)}, u32[]{:S(2)}, u32[]{:S(2)}) collective-permute-start(bf16[192,384]{1,0:T(8,128)(2,1)S(1)} %get-tuple-element.146), channel_id=1, source_target_pairs={{0,16},{8,24},{16,0},{24,8},{1,17},{9,25},{17,1},{25,9},{2,18},{10... | collective-permute-start | bytes 442376 | tf_op jit(solution)/shard_map/ppermute | solution.py:19
  91.8 13.1 %collective-permute-start.16 = (bf16[192,384]{1,0:T(8,128)(2,1)S(1)}, bf16[192,384]{1,0:T(8,128)(2,1)S(1)}, u32[]{:S(2)}, u32[]{:S(2)}) collective-permute-start(bf16[192,384]{1,0:T(8,128)(2,1)S(1)} %get-tuple-element.145), channel_id=1, source_target_pairs={{0,24},{8,16},{16,8},{24,0},{1,25},{9,17},{17,9},{25,1},{2,26},{10... | collective-permute-start | bytes 442376 | tf_op jit(solution)/shard_map/ppermute | solution.py:19
  105.7 16.5 %collective-permute-start.17 = (bf16[192,384]{1,0:T(8,128)(2,1)S(1)}, bf16[192,384]{1,0:T(8,128)(2,1)S(1)}, u32[]{:S(2)}, u32[]{:S(2)}) collective-permute-start(bf16[192,384]{1,0:T(8,128)(2,1)S(1)} %get-tuple-element.116), channel_id=1, source_target_pairs={{0,8},{8,0},{16,24},{24,16},{1,9},{9,1},{17,25},{25,17},{2,10},{10... | collective-permute-start | bytes 442376 | tf_op jit(solution)/shard_map/ppermute | solution.py:19
  109.1 13.1 %collective-permute-start.18 = (bf16[192,384]{1,0:T(8,128)(2,1)S(1)}, bf16[192,384]{1,0:T(8,128)(2,1)S(1)}, u32[]{:S(2)}, u32[]{:S(2)}) collective-permute-start(bf16[192,384]{1,0:T(8,128)(2,1)S(1)} %get-tuple-element.116), channel_id=1, source_target_pairs={{0,16},{8,24},{16,0},{24,8},{1,17},{9,25},{17,1},{25,9},{2,18},{10... | collective-permute-start | bytes 442376 | tf_op jit(solution)/shard_map/ppermute | solution.py:19
  109.1 13.1 %collective-permute-start.19 = (bf16[192,384]{1,0:T(8,128)(2,1)S(1)}, bf16[192,384]{1,0:T(8,128)(2,1)S(1)}, u32[]{:S(2)}, u32[]{:S(2)}) collective-permute-start(bf16[192,384]{1,0:T(8,128)(2,1)S(1)} %get-tuple-element.116), channel_id=1, source_target_pairs={{0,24},{8,16},{16,8},{24,0},{1,25},{9,17},{17,9},{25,1},{2,26},{10... | collective-permute-start | bytes 442376 | tf_op jit(solution)/shard_map/ppermute | solution.py:19
  111.6 9.7 %collective-permute-start.20 = (f32[192,192]{1,0:T(8,128)S(1)}, f32[192,192]{1,0:T(8,128)S(1)}, u32[]{:S(2)}, u32[]{:S(2)}) collective-permute-start(f32[192,192]{1,0:T(8,128)S(1)} %get-tuple-element.115), channel_id=1, source_target_pairs={{0,4},{4,0},{1,5},{5,1},{2,6},{6,2},{3,7},{7,3},{8,12},{12,8},{9,1... | collective-permute-start | bytes 442376 | tf_op jit(solution)/shard_map/ppermute | solution.py:19
  122.3 8.2 %collective-permute-start.23 = (bf16[384,384]{1,0:T(8,128)(2,1)S(1)}, bf16[384,384]{1,0:T(8,128)(2,1)S(1)}, u32[]{:S(2)}, u32[]{:S(2)}) collective-permute-start(bf16[384,384]{1,0:T(8,128)(2,1)S(1)} %constant_dynamic-update-slice_fusion.2.refs_4_), channel_id=1, source_target_pairs={{0,2},{1,3},{2,0},{3,1},{4,6},{5,7},{6,4},{7,5},{8,10},{9,11},{10,... | collective-permute-start | bytes 884744 | tf_op jit(solution)/shard_map/ppermute | solution.py:19
  123.9 7.7 %collective-permute-start.22 = (bf16[384,384]{1,0:T(8,128)(2,1)S(1)}, bf16[384,384]{1,0:T(8,128)(2,1)S(1)}, u32[]{:S(2)}, u32[]{:S(2)}) collective-permute-start(bf16[384,384]{1,0:T(8,128)(2,1)S(1)} %constant_dynamic-update-slice_fusion.refs_0_), channel_id=1, source_target_pairs={{0,4},{4,0},{1,5},{5,1},{2,6},{6,2},{3,7},{7,3},{8,12},{12,8},{9,1... | collective-permute-start | bytes 884744 | tf_op jit(solution)/shard_map/ppermute | solution.py:19
  125.2 19.1 %collective-permute-start.24 = (bf16[3,192,384]{2,1,0:T(8,128)(2,1)S(1)}, bf16[3,192,384]{2,1,0:T(8,128)(2,1)S(1)}, u32[]{:S(2)}, u32[]{:S(2)}) collective-permute-start(bf16[3,192,384]{2,1,0:T(8,128)(2,1)S(1)} %get-tuple-element.121), channel_id=1, source_target_pairs={{0,8},{8,0},{16,24},{24,16},{1,9},{9,1},{17,25},{25,17},{2,10},{10... | collective-permute-start | bytes 1327112 | tf_op jit(solution)/shard_map/ppermute | solution.py:19
  128.2 33.0 %collective-permute-start.28 = (bf16[3,192,384]{2,1,0:T(8,128)(2,1)S(1)}, bf16[3,192,384]{2,1,0:T(8,128)(2,1)S(1)}, u32[]{:S(2)}, u32[]{:S(2)}) collective-permute-start(bf16[3,192,384]{2,1,0:T(8,128)(2,1)S(1)} %get-tuple-element.126), channel_id=1, source_target_pairs={{0,16},{8,24},{16,0},{24,8},{1,17},{9,25},{17,1},{25,9},{2,18},{10... | collective-permute-start | bytes 1327112 | tf_op jit(solution)/shard_map/ppermute | solution.py:19
  128.2 33.0 %collective-permute-start.29 = (bf16[3,192,384]{2,1,0:T(8,128)(2,1)S(1)}, bf16[3,192,384]{2,1,0:T(8,128)(2,1)S(1)}, u32[]{:S(2)}, u32[]{:S(2)}) collective-permute-start(bf16[3,192,384]{2,1,0:T(8,128)(2,1)S(1)} %get-tuple-element.127), channel_id=1, source_target_pairs={{0,24},{8,16},{16,8},{24,0},{1,25},{9,17},{17,9},{25,1},{2,26},{10... | collective-permute-start | bytes 1327112 | tf_op jit(solution)/shard_map/ppermute | solution.py:19
  130.5 14.5 %collective-permute-start.26 = (bf16[384,384]{1,0:T(8,128)(2,1)S(1)}, bf16[384,384]{1,0:T(8,128)(2,1)S(1)}, u32[]{:S(2)}, u32[]{:S(2)}) collective-permute-start(bf16[384,384]{1,0:T(8,128)(2,1)S(1)} %constant_dynamic-update-slice_fusion.2.refs_4_), channel_id=1, source_target_pairs={{0,4},{4,0},{1,5},{5,1},{2,6},{6,2},{3,7},{7,3},{8,12},{12,8},{9,1... | collective-permute-start | bytes 884744 | tf_op jit(solution)/shard_map/ppermute | solution.py:19
  131.6 14.1 %collective-permute-start.21 = (bf16[384,384]{1,0:T(8,128)(2,1)S(1)}, bf16[384,384]{1,0:T(8,128)(2,1)S(1)}, u32[]{:S(2)}, u32[]{:S(2)}) collective-permute-start(bf16[384,384]{1,0:T(8,128)(2,1)S(1)} %constant_dynamic-update-slice_fusion.refs_0_), channel_id=1, source_target_pairs={{0,2},{1,3},{2,0},{3,1},{4,6},{5,7},{6,4},{7,5},{8,10},{9,11},{10,... | collective-permute-start | bytes 884744 | tf_op jit(solution)/shard_map/ppermute | solution.py:19
  144.4 17.3 %collective-permute-start.25 = (bf16[384,384]{1,0:T(8,128)(2,1)S(1)}, bf16[384,384]{1,0:T(8,128)(2,1)S(1)}, u32[]{:S(2)}, u32[]{:S(2)}) collective-permute-start(bf16[384,384]{1,0:T(8,128)(2,1)S(1)} %collective-permute-done.22.refs_1_), channel_id=1, source_target_pairs={{0,2},{1,3},{2,0},{3,1},{4,6},{5,7},{6,4},{7,5},{8,10},{9,11},{10,... | collective-permute-start | bytes 884744 | tf_op jit(solution)/shard_map/ppermute | solution.py:19
  145.0 16.7 %collective-permute-start.27 = (bf16[384,384]{1,0:T(8,128)(2,1)S(1)}, bf16[384,384]{1,0:T(8,128)(2,1)S(1)}, u32[]{:S(2)}, u32[]{:S(2)}) collective-permute-start(bf16[384,384]{1,0:T(8,128)(2,1)S(1)} %collective-permute-done.23.refs_5_), channel_id=1, source_target_pairs={{0,4},{4,0},{1,5},{5,1},{2,6},{6,2},{3,7},{7,3},{8,12},{12,8},{9,1... | collective-permute-start | bytes 884744 | tf_op jit(solution)/shard_map/ppermute | solution.py:19
  145.7 16.5 %collective-permute-start.34 = (bf16[384,384]{1,0:T(8,128)(2,1)S(1)}, bf16[384,384]{1,0:T(8,128)(2,1)S(1)}, u32[]{:S(2)}, u32[]{:S(2)}) collective-permute-start(bf16[384,384]{1,0:T(8,128)(2,1)S(1)} %constant_dynamic-update-slice_fusion.2.refs_4_), channel_id=1, source_target_pairs={{0,1},{1,0},{2,3},{3,2},{4,5},{5,4},{6,7},{7,6},{8,9},{9,8},{10,11... | collective-permute-start | bytes 884744 | tf_op jit(solution)/shard_map/ppermute | solution.py:19
  161.1 1.6 collective-permute-start.30
  161.1 2.0 %collective-permute-start.31 = (bf16[384,384]{1,0:T(8,128)(2,1)S(1)}, bf16[384,384]{1,0:T(8,128)(2,1)S(1)}, u32[]{:S(2)}, u32[]{:S(2)}) collective-permute-start(bf16[384,384]{1,0:T(8,128)(2,1)S(1)} %collective-permute-done.22.refs_1_), channel_id=1, source_target_pairs={{0,1},{1,0},{2,3},{3,2},{4,5},{5,4},{6,7},{7,6},{8,9},{9,8},{10,11... | collective-permute-start | bytes 884744 | tf_op jit(solution)/shard_map/ppermute | solution.py:19
  161.6 2.6 %collective-permute-start.35 = (bf16[384,384]{1,0:T(8,128)(2,1)S(1)}, bf16[384,384]{1,0:T(8,128)(2,1)S(1)}, u32[]{:S(2)}, u32[]{:S(2)}) collective-permute-start(bf16[384,384]{1,0:T(8,128)(2,1)S(1)} %collective-permute-done.23.refs_5_), channel_id=1, source_target_pairs={{0,1},{1,0},{2,3},{3,2},{4,5},{5,4},{6,7},{7,6},{8,9},{9,8},{10,11... | collective-permute-start | bytes 884744 | tf_op jit(solution)/shard_map/ppermute | solution.py:19
  161.7 3.4 %collective-permute-start.32 = (bf16[384,384]{1,0:T(8,128)(2,1)S(1)}, bf16[384,384]{1,0:T(8,128)(2,1)S(1)}, u32[]{:S(2)}, u32[]{:S(2)}) collective-permute-start(bf16[384,384]{1,0:T(8,128)(2,1)S(1)} %collective-permute-done.21.refs_2_), channel_id=1, source_target_pairs={{0,1},{1,0},{2,3},{3,2},{4,5},{5,4},{6,7},{7,6},{8,9},{9,8},{10,11... | collective-permute-start | bytes 884744 | tf_op jit(solution)/shard_map/ppermute | solution.py:19
  162.2 10.9 %collective-permute-start.33 = (bf16[384,384]{1,0:T(8,128)(2,1)S(1)}, bf16[384,384]{1,0:T(8,128)(2,1)S(1)}, u32[]{:S(2)}, u32[]{:S(2)}) collective-permute-start(bf16[384,384]{1,0:T(8,128)(2,1)S(1)} %collective-permute-done.25.refs_3_), channel_id=1, source_target_pairs={{0,1},{1,0},{2,3},{3,2},{4,5},{5,4},{6,7},{7,6},{8,9},{9,8},{10,11... | collective-permute-start | bytes 884744 | tf_op jit(solution)/shard_map/ppermute | solution.py:19
  162.7 10.4 %collective-permute-start.36 = (bf16[384,384]{1,0:T(8,128)(2,1)S(1)}, bf16[384,384]{1,0:T(8,128)(2,1)S(1)}, u32[]{:S(2)}, u32[]{:S(2)}) collective-permute-start(bf16[384,384]{1,0:T(8,128)(2,1)S(1)} %collective-permute-done.26.refs_6_), channel_id=1, source_target_pairs={{0,1},{1,0},{2,3},{3,2},{4,5},{5,4},{6,7},{7,6},{8,9},{9,8},{10,11... | collective-permute-start | bytes 884744 | tf_op jit(solution)/shard_map/ppermute | solution.py:19
  163.1 10.0 %collective-permute-start.37 = (bf16[384,384]{1,0:T(8,128)(2,1)S(1)}, bf16[384,384]{1,0:T(8,128)(2,1)S(1)}, u32[]{:S(2)}, u32[]{:S(2)}) collective-permute-start(bf16[384,384]{1,0:T(8,128)(2,1)S(1)} %collective-permute-done.27.refs_7_), channel_id=1, source_target_pairs={{0,1},{1,0},{2,3},{3,2},{4,5},{5,4},{6,7},{7,6},{8,9},{9,8},{10,11... | collective-permute-start | bytes 884744 | tf_op jit(solution)/shard_map/ppermute | solution.py:19
  164.3 15.2 %collective-permute-start.38 = (f32[192,192]{1,0:T(8,128)S(1)}, f32[192,192]{1,0:T(8,128)S(1)}, u32[]{:S(2)}, u32[]{:S(2)}) collective-permute-start(f32[192,192]{1,0:T(8,128)S(1)} %get-tuple-element.138), channel_id=1, source_target_pairs={{0,4},{4,0},{1,5},{5,1},{2,6},{6,2},{3,7},{7,3},{8,12},{12,8},{9,1... | collective-permute-start | bytes 442376 | tf_op jit(solution)/shard_map/ppermute | solution.py:19
  165.1 14.4 %collective-permute-start.39 = (bf16[192,384]{1,0:T(8,128)(2,1)S(1)}, bf16[192,384]{1,0:T(8,128)(2,1)S(1)}, u32[]{:S(2)}, u32[]{:S(2)}) collective-permute-start(bf16[192,384]{1,0:T(8,128)(2,1)S(1)} %get-tuple-element.139), channel_id=1, source_target_pairs={{0,0},{1,8},{2,16},{3,24},{4,4},{5,12},{6,20},{7,28},{8,1},{9,9},{... | collective-permute-start | bytes 442376 | tf_op jit(solution)/shard_map/ppermute | solution.py:734
  (6 other events, 62.5 us)
